TPU v7x, 256 devices: a whole 4x4x8 slice. The times are simulated.
256 devices in a mesh: img: 8 (over z_hi, x), cap: 16 (over y, z_lo), chip: 2 (over core).
Axes of the slice: x: 4, y: 4, z: 8 (z_hi: 2, z_lo: 4; z = z_hi * 4 + z_lo), core: 2. Of those that a mesh axis runs over, the one named last changes fastest.
Arguments:
- teacher_img: float32 [16, 16, 64, 1280], P(('img', 'chip'), 'cap'), may hold values from -4096 to 4096
- teacher_cap: float32 [16, 16, 64, 1280], P('cap', ('img', 'chip')), may hold values from -4096 to 4096
- student_img: bfloat16 [16, 16, 64, 512], P(('img', 'chip'), 'cap'), may hold values from -4096 to 4096
- student_cap: bfloat16 [16, 16, 64, 512], P('cap', ('img', 'chip')), may hold values from -4096 to 4096
Outputs:
- grad_img: float32 [16, 16, 64, 512], P(('img', 'chip'), 'cap')
- grad_cap: float32 [16, 16, 64, 512], P('cap', ('img', 'chip'))
All inputs are finite; a program needn't handle non-finite values.
Results may differ from a plain program's by a relative error of at most 0.0023.
Values may be sent and summed in bfloat16 or wider, within the bound.
No kernel may reach another device: no remote copies, remote signals or barrier semaphores. Data moves between devices by JAX's collectives and lax.ppermute only.
A program may use at most 64 MiB of HBM per device.

v0:
```python
import math

import jax
import jax.numpy as jnp
from jax import lax
from jax.experimental import pallas as pl
from jax.experimental.pallas import tpu as pltpu
from jax.sharding import Mesh, PartitionSpec as P

LOG2E = math.log2(math.e)
teacher_scale = 0.0625 * LOG2E
student_scale = 0.125 * LOG2E
weight_scale = 0.125 * 0.5
PLANE = ("x", "y")
RING = ("zh", "zl")
BF16 = jnp.bfloat16
F32 = jnp.float32
MIB = 1024 * 1024
VMEM = pl.BlockSpec(memory_space=pltpu.VMEM)


def nt(a, b):
    return lax.dot_general(a, b, (((1,), (1,)), ((), ())), preferred_element_type=F32)


def tn(a, b):
    return lax.dot_general(a, b, (((0,), (0,)), ((), ())), preferred_element_type=F32)


def log2_sum(tile, axis):
    peak = jnp.max(tile, axis=axis, keepdims=True)
    total = jnp.sum(jnp.exp2(tile - peak), axis=axis, keepdims=True)
    return peak + jnp.log(total) * LOG2E


def join(a, b):
    return jnp.maximum(a, b) + jnp.log1p(jnp.exp2(-jnp.abs(a - b))) * LOG2E


def split(t, s, out_ref, order):
    width = t.shape[1]
    hi = t.astype(BF16)
    parts = {"high": hi, "low": (t - hi.astype(F32)).astype(BF16)}
    for i, name in enumerate(order):
        out_ref[:, i * width : (i + 1) * width] = parts[name]
    out_ref[:, 2 * width :] = s


def pack_rows(t, s):
    def kernel(t_ref, s_ref, out_ref):
        split(t_ref[...], s_ref[...], out_ref, ("high", "low"))

    return pl.pallas_call(
        kernel,
        out_shape=jax.ShapeDtypeStruct((t.shape[0], 2 * t.shape[1] + s.shape[1]), BF16),
        compiler_params=pltpu.CompilerParams(vmem_limit_bytes=16 * MIB),
        name="pack_rows",
    )(t, s)


def pack_cols(t, s, t_other, s_other):
    def kernel(t_ref, s_ref, t_other_ref, s_other_ref, out_ref):
        split(t_ref[...], s_ref[...], out_ref.at[0], ("low", "high"))
        split(t_other_ref[...], s_other_ref[...], out_ref.at[1], ("low", "high"))

    return pl.pallas_call(
        kernel,
        out_shape=jax.ShapeDtypeStruct((2, t.shape[0], 2 * t.shape[1] + s.shape[1]), BF16),
        compiler_params=pltpu.CompilerParams(vmem_limit_bytes=16 * MIB),
        name="pack_cols",
    )(t, s, t_other, s_other)


def row_plan(x, y, sign, share):
    half = share // 2

    def at(p, q, part=0):
        chip_x = lax.rem(x - sign * p + 8, 4)
        chip_y = lax.rem(y - sign * q + 8, 4)
        return (chip_x * 4 + chip_y) * share + part * half

    plan = []

    def add(piece, *parts):
        first = 0
        for p, q, part in parts:
            size = share if part is None else half
            plan.append((piece, first, size, at(p, q, part or 0)))
            first += size

    add(0, (0, 0, None))
    add(1, (1, 0, None))
    add(2, (3, 0, None))
    add(3, (0, 1, None))
    add(4, (0, 3, None))
    add(5, (2, 0, None), (1, 1, 1), (1, 3, 1))
    add(6, (3, 1, 1), (3, 3, 1))
    add(7, (0, 2, None), (1, 1, 0), (3, 1, 0))
    add(8, (1, 3, 0), (3, 3, 0))
    add(9, (2, 1, 1), (2, 3, 1), (1, 2, 1))
    add(10, (3, 2, 1))
    add(11, (1, 2, 0), (3, 2, 0), (2, 1, 0))
    add(12, (2, 3, 0))
    add(13, (2, 2, 1))
    add(14, (2, 2, 0))
    return plan


def col_plan(z, sign, share, ring):
    half = ring // 2
    plan = []
    for k in range(half):
        behind = lax.rem(z - sign * k + ring, ring) * share
        plan += [(k, 0, behind), (k, 1, ring * share + behind)]
        if k:
            ahead = lax.rem(z + sign * k + ring, ring) * share
            plan += [(half + k - 1, 1, ahead), (half + k - 1, 0, ring * share + ahead)]
    far = lax.rem(z + half, ring) * share
    plan += [(2 * half - 1, None, far), (2 * half, None, ring * share + far)]
    return plan


def logits(row_pieces, col_pieces, width, share, ring):
    m = 16 * share
    n = 2 * ring * share
    total = row_pieces[0].shape[1]
    ds = total - 2 * width
    tile = 256
    n_rows = len(row_pieces)
    n_cols = len(col_pieces)

    def kernel(*refs):
        rows_in = refs[:n_rows]
        cols_in = refs[n_rows : n_rows + n_cols]
        refs = refs[n_rows + n_cols :]
        t_ref, s_ref, row_ref, col_ref, srow_ref, scol_ref, r_buf, c_buf = refs
        x, y, z = lax.axis_index("x"), lax.axis_index("y"), lax.axis_index(RING)
        sign = 1 - 2 * lax.axis_index("core")

        def place(src, first, buf, at, size):
            def some_rows(i, _):
                there = pl.ds(pl.multiple_of(at + 16 * i, 16), 16)
                buf[there, :] = src[pl.ds(pl.multiple_of(first + 16 * i, 16), 16), :]
                return 0

            lax.fori_loop(0, size // 16, some_rows, 0)

        for piece, first, size, at in row_plan(x, y, sign, share):
            place(rows_in[piece], first, r_buf, at, size)
        for piece, part, at in col_plan(z, sign, share, ring):
            place(cols_in[piece] if part is None else cols_in[piece].at[part], 0, c_buf, at, share)

        def columns(j, _):
            here = pl.ds(pl.multiple_of(j * tile, tile), tile)
            teacher = teacher_scale * (
                nt(r_buf[:, : 2 * width], c_buf[here, : 2 * width])
                + nt(r_buf[:, :width], c_buf[here, width : 2 * width])
            )
            student = student_scale * nt(r_buf[:, 2 * width :], c_buf[here, 2 * width :])
            for k, (value, ref) in enumerate(((teacher, t_ref), (student, s_ref))):
                ref[:, here] = value
                col_ref[k : k + 1, here] = log2_sum(value, 0)
            return 0

        lax.fori_loop(0, n // tile, columns, 0)
        lanes = lax.broadcasted_iota(jnp.int32, (128, 128), 1)

        def row_sums(i, _):
            here = pl.ds(pl.multiple_of(i * 128, 128), 128)
            teacher = log2_sum(t_ref[here, :], 1)
            student = log2_sum(s_ref[here, :], 1)
            both = jnp.transpose(jnp.where(lanes == 0, teacher, student))
            row_ref[:, here] = both[:2, :]
            srow_ref[here, :] = r_buf[here, 2 * width :]
            scol_ref[here, :] = c_buf[here, 2 * width :]
            return 0

        lax.fori_loop(0, m // 128, row_sums, 0)

    return pl.pallas_call(
        kernel,
        in_specs=[VMEM] * (n_rows + n_cols),
        out_specs=[VMEM] * 6,
        out_shape=[
            jax.ShapeDtypeStruct((m, n), F32),
            jax.ShapeDtypeStruct((m, n), F32),
            jax.ShapeDtypeStruct((2, m), F32),
            jax.ShapeDtypeStruct((2, n), F32),
            jax.ShapeDtypeStruct((m, ds), BF16),
            jax.ShapeDtypeStruct((n, ds), BF16),
        ],
        scratch_shapes=[
            pltpu.VMEM((m, total), BF16),
            pltpu.VMEM((n, total), BF16),
        ],
        compiler_params=pltpu.CompilerParams(vmem_limit_bytes=28 * MIB),
        cost_estimate=pl.CostEstimate(
            flops=2 * m * n * (3 * width + ds),
            bytes_accessed=2 * (m + n) * total + 8 * m * n,
            transcendentals=4 * m * n,
        ),
        name="logits",
    )(*row_pieces, *col_pieces)


def weights(t, s, row_lse, col_lse, srow, share, ring):
    m, n = t.shape
    ds = srow.shape[1]
    block = 512

    def kernel(
        t_ref, s_ref, row_ref, col_ref, srow_ref, w_ref, mine_ref, theirs_ref, lse, acc
    ):
        step = pl.program_id(0)

        @pl.when(step == 0)
        def _():
            lse[...] = jnp.transpose(
                jnp.concatenate([row_ref[...], jnp.zeros((126, m), F32)], axis=0)
            )

        t = t_ref[...]
        s = s_ref[...]
        row = lse[pl.ds(pl.multiple_of(step * block, block), block), :]
        along_rows = jnp.exp2(s - row[:, 1:2]) - jnp.exp2(t - row[:, 0:1])
        along_cols = jnp.exp2(s - col_ref[1:2, :]) - jnp.exp2(t - col_ref[0:1, :])
        w = (weight_scale * (along_rows + along_cols)).astype(BF16)
        w_ref[...] = w
        part = tn(w, srow_ref[...])

        @pl.when(step == 0)
        def _():
            acc[...] = part

        @pl.when(step > 0)
        def _():
            acc[...] += part

        @pl.when(step == pl.num_programs(0) - 1)
        def _():
            z = lax.axis_index(RING)
            sign = 1 - 2 * lax.axis_index("core")

            def terms(ahead, other):
                at = lax.rem(z + ahead + ring, ring) * share + other * ring * share
                return acc[pl.ds(pl.multiple_of(at, share), share), :]

            half = ring // 2
            slots = [(k, h) for k in range(1, half) for h in (0, 1)]
            for i, (k, h) in enumerate(slots):
                here = slice(i * share, (i + 1) * share)
                mine_ref[here, :] = terms(sign * k, h)
                theirs_ref[here, :] = terms(-sign * k, 1 - h)
            for i, k in enumerate((half, 0)):
                here = slice((ring - 2 + i) * share, (ring - 1 + i) * share)
                mine_ref[here, :] = terms(k, 0)
                theirs_ref[here, :] = terms(k, 1)

    return pl.pallas_call(
        kernel,
        grid=(m // block,),
        in_specs=[
            pl.BlockSpec((block, n), lambda i: (i, 0)),
            pl.BlockSpec((block, n), lambda i: (i, 0)),
            pl.BlockSpec((2, m), lambda i: (0, 0)),
            pl.BlockSpec((2, n), lambda i: (0, 0)),
            pl.BlockSpec((block, ds), lambda i: (i, 0)),
        ],
        out_specs=[
            pl.BlockSpec((block, n), lambda i: (i, 0)),
            pl.BlockSpec((n // 2, ds), lambda i: (0, 0)),
            pl.BlockSpec((n // 2, ds), lambda i: (0, 0)),
        ],
        out_shape=[
            jax.ShapeDtypeStruct((m, n), BF16),
            jax.ShapeDtypeStruct((n // 2, ds), F32),
            jax.ShapeDtypeStruct((n // 2, ds), F32),
        ],
        scratch_shapes=[pltpu.VMEM((m, 128), F32), pltpu.VMEM((n, ds), F32)],
        compiler_params=pltpu.CompilerParams(vmem_limit_bytes=20 * MIB),
        cost_estimate=pl.CostEstimate(
            flops=2 * m * n * ds, bytes_accessed=10 * m * n, transcendentals=4 * m * n
        ),
        name="weights",
    )(t, s, row_lse, col_lse, srow)


def img_terms(w, scol):
    m, n = w.shape
    ds = scol.shape[1]
    block = 512

    def kernel(w_ref, scol_ref, img_ref):
        img_ref[...] = jnp.dot(w_ref[...], scol_ref[...], preferred_element_type=F32).astype(BF16)

    return pl.pallas_call(
        kernel,
        grid=(m // block,),
        in_specs=[
            pl.BlockSpec((block, n), lambda i: (i, 0)),
            pl.BlockSpec((n, ds), lambda i: (0, 0)),
        ],
        out_specs=pl.BlockSpec((block, ds), lambda i: (i, 0)),
        out_shape=jax.ShapeDtypeStruct((m, ds), BF16),
        compiler_params=pltpu.CompilerParams(vmem_limit_bytes=10 * MIB),
        cost_estimate=pl.CostEstimate(
            flops=2 * m * n * ds, bytes_accessed=4 * m * n, transcendentals=0
        ),
        name="img_terms",
    )(w, scol)


def deal(mine, came, share, ring):
    ds = mine.shape[1]
    sizes = [2 * share] * (ring // 2 - 1) + [share]

    def kernel(mine_ref, came_ref, *out_refs):
        first = 0
        for size, ref in zip(sizes + [share], out_refs):
            here = slice(first, first + size)
            ref[...] = (mine_ref[here, :] + came_ref[here, :]).astype(ref.dtype)
            first += size

    return pl.pallas_call(
        kernel,
        in_specs=[VMEM, VMEM],
        out_specs=[VMEM] * (len(sizes) + 1),
        out_shape=[jax.ShapeDtypeStruct((size, ds), BF16) for size in sizes]
        + [jax.ShapeDtypeStruct((share, ds), F32)],
        compiler_params=pltpu.CompilerParams(vmem_limit_bytes=10 * MIB),
        name="deal",
    )(mine, came)


def swap(x):
    return lax.ppermute(x, "core", [(0, 1), (1, 0)])


def turn(x, axis, step):
    n = lax.axis_size(axis)
    axes = (axis if isinstance(axis, tuple) else (axis,)) + ("core",)
    pairs = [(2 * i + c, 2 * ((i + (step, -step)[c]) % n) + c) for i in range(n) for c in (0, 1)]
    return lax.ppermute(x, axes, pairs)


def join_along(x, axis, step):
    n = lax.axis_size(axis)
    return join(x, lax.ppermute(x, axis, [(i, i ^ step) for i in range(n)]))


def gather(r, c0, share):
    hold = lax.optimization_barrier
    half = share // 2
    a = lambda v: v[:half]
    b = lambda v: v[half : 2 * half]
    cat = lambda *v: jnp.concatenate(v, axis=0)
    x1, x1r, y1, y1r, c1 = hold(
        (turn(r, "x", 1), turn(r, "x", -1), turn(r, "y", 1), turn(r, "y", -1), turn(c0, RING, 1))
    )
    bx = cat(b(y1), b(y1r))
    ay = cat(a(x1), a(x1r))
    d1, c1 = hold((swap(c1), c1))
    x2, x2r, y2, y2r, c2, d1 = hold(
        (
            turn(cat(x1, bx), "x", 1),
            turn(bx, "x", -1),
            turn(cat(y1, ay), "y", 1),
            turn(ay, "y", -1),
            turn(c1, RING, 1),
            d1,
        )
    )
    x3, x3r, y3, y3r, c3 = hold(
        (
            turn(cat(x2[share:], b(y2)), "x", 1),
            turn(b(y2), "x", -1),
            turn(cat(y2[share:], a(x2)), "y", 1),
            turn(a(x2), "y", -1),
            turn(c2, RING, 1),
        )
    )
    x4, y4, c4, d2, c3 = hold(
        (turn(x3[share:], "x", 1), turn(y3[share:], "y", 1), turn(c3[0], RING, 1), swap(c2), c3)
    )
    rows = [r, x1, x1r, y1, y1r, x2, x2r, y2, y2r, x3, x3r, y3, y3r, x4, y4]
    return rows, [c0, c1, c2, c3, d1, d2, swap(c3), c4, swap(c4)]


def local(teacher_img, teacher_cap, student_img, student_cap):
    width = teacher_img.shape[3]
    share, ds = student_img.shape[2:]
    ring = lax.axis_size(RING)
    rows_own = pack_rows(teacher_img[0, 0], student_img[0, 0])
    cols_own = (teacher_cap[0, 0], student_cap[0, 0])
    cols_pair = pack_cols(*cols_own, *[swap(v) for v in cols_own])
    rows, cols = gather(rows_own, cols_pair, share)
    t, s, row_lse, col_lse, srow, scol = logits(rows, cols, width, share, ring)

    came = swap(col_lse)
    half = ring * share
    col_lse = join(col_lse, jnp.concatenate([came[:, half:], came[:, :half]], axis=1))
    for step in (1, 2, 4):
        col_lse = join_along(col_lse, RING, step)
    for axis in PLANE:
        for step in (1, 3):
            row_lse = join_along(row_lse, axis, step)

    w, mine, theirs = weights(t, s, row_lse, col_lse, srow, share, ring)
    img_sent = lax.all_to_all(img_terms(w, scol).reshape(-1, share, ds), PLANE, 0, 0)
    *dealt, own = deal(mine, swap(theirs), share, ring)
    other = None
    for k, terms in enumerate(dealt, 1):
        terms = turn(terms, RING, k).astype(F32)
        own = own + terms[:share]
        if terms.shape[0] > share:
            other = terms[share:] if other is None else other + terms[share:]
    grad_cap = own + swap(other)
    grad_img = jnp.sum(img_sent.astype(F32), axis=0)
    return grad_img[None, None], grad_cap[None, None]


def solution(mesh):
    fine = Mesh(mesh.devices.reshape(2, 4, 4, 4, 2), ("zh", "x", "y", "zl", "core"))
    img = P(("zh", "x", "core"), ("y", "zl"), None, None)
    cap = P(("y", "zl"), ("zh", "x", "core"), None, None)
    return jax.shard_map(
        local,
        mesh=fine,
        in_specs=(img, cap, img, cap),
        out_specs=(img, cap),
        check_vma=False,
    )
```

profile of v0, /device:TPU:1, one launch (start us, length us, event | category | flops | bytes accessed | tf_op | source)
XLA Modules:
  0.0 141.4 jit_solution(7156053554235439194)
XLA Ops:
  0.6 3.3 %collective-permute-start.4 = (f32[64,1280]{1,0:T(8,128)}, f32[64,1280]{1,0:T(8,128)S(1)}, u32[]{:S(2)}, u32[]{:S(2)}) collective-permute-start(f32[64,1280]{1,0:T(8,128)} %bitcast.11), channel_id=1, source_target_pairs={{0,1},{1,0},{2,3},{3,2},{4,5},{5,4},{6,7},{7,6},{8,9},{9,8},{10,11... | collective-permute-start | bytes 983048 | tf_op jit(solution)/shard_map/ppermute | solution.py:336
  7.4 3.9 %collective-permute-start.6 = (bf16[2,64,3072]{2,1,0:T(8,128)(2,1)S(1)}, bf16[2,64,3072]{2,1,0:T(8,128)(2,1)S(1)}, u32[]{:S(2)}, u32[]{:S(2)}) collective-permute-start(bf16[2,64,3072]{2,1,0:T(8,128)(2,1)S(1)} %pack_cols.1.refs_15_), channel_id=1, source_target_pairs={{0,2},{1,135},{2,4},{3,1},{4,6},{5,3},{6,128},{7,5},{128,130},{129... | collective-permute-start | bytes 2359304 | tf_op jit(solution)/shard_map/ppermute | solution.py:343
  17.0 6.8 %collective-permute-done.3.refs_4_ = bf16[64,3072]{1,0:T(8,128)(2,1)S(1)} collective-permute-done((bf16[64,3072]{1,0:T(8,128)(2,1)S(1)}, bf16[64,3072]{1,0:T(8,128)(2,1)S(1)}, u32[]{:S(2)}, u32[]{:S(2)}) %collective-permute-start.3) | collective-permute-done | bytes 393248 | tf_op jit(solution)/shard_map/ppermute | solution.py:343
  23.8 2.8 %collective-permute-done.1.refs_2_ = bf16[64,3072]{1,0:T(8,128)(2,1)S(1)} collective-permute-done((bf16[64,3072]{1,0:T(8,128)(2,1)S(1)}, bf16[64,3072]{1,0:T(8,128)(2,1)S(1)}, u32[]{:S(2)}, u32[]{:S(2)}) %collective-permute-start.1) | collective-permute-done | bytes 393248 | tf_op jit(solution)/shard_map/ppermute | solution.py:343
  29.6 2.6 %collective-permute-start.12 = (bf16[2,64,3072]{2,1,0:T(8,128)(2,1)S(1)}, bf16[2,64,3072]{2,1,0:T(8,128)(2,1)S(1)}, u32[]{:S(2)}, u32[]{:S(2)}) collective-permute-start(bf16[2,64,3072]{2,1,0:T(8,128)(2,1)S(1)} %collective-permute-done.6.refs_16_), channel_id=1, source_target_pairs={{0,2},{1,135},{2,4},{3,1},{4,6},{5,3},{6,128},{7,5},{128,130},{129... | collective-permute-start | bytes 2359304 | tf_op jit(solution)/shard_map/ppermute | solution.py:343
  32.5 11.9 %collective-permute-done.10.refs_8_ = bf16[64,3072]{1,0:T(8,128)(2,1)S(1)} collective-permute-done((bf16[64,3072]{1,0:T(8,128)(2,1)S(1)}, bf16[64,3072]{1,0:T(8,128)(2,1)S(1)}, u32[]{:S(2)}, u32[]{:S(2)}) %collective-permute-start.10) | collective-permute-done | bytes 393248 | tf_op jit(solution)/shard_map/ppermute | solution.py:343
  44.7 3.0 %collective-permute-start.15 = (bf16[96,3072]{1,0:T(8,128)(2,1)S(1)}, bf16[96,3072]{1,0:T(8,128)(2,1)S(1)}, u32[]{:S(2)}, u32[]{:S(2)}) collective-permute-start(bf16[96,3072]{1,0:T(8,128)(2,1)S(1)} %pad_maximum_fusion.3), channel_id=1, source_target_pairs={{0,8},{1,25},{8,16},{9,1},{16,24},{17,9},{24,0},{25,17},{2,10},{3,... | collective-permute-start | bytes 1769480 | tf_op jit(solution)/shard_map/ppermute | solution.py:343
  50.1 7.3 %collective-permute-done.14.refs_10_ = bf16[32,3072]{1,0:T(8,128)(2,1)S(1)} collective-permute-done((bf16[32,3072]{1,0:T(8,128)(2,1)S(1)}, bf16[32,3072]{1,0:T(8,128)(2,1)S(1)}, u32[]{:S(2)}, u32[]{:S(2)}) %collective-permute-start.14) | collective-permute-done | bytes 196640 | tf_op jit(solution)/shard_map/ppermute | solution.py:343
  61.0 2.6 %collective-permute-start.18 = (bf16[32,3072]{1,0:T(8,128)(2,1)S(1)}, bf16[32,3072]{1,0:T(8,128)(2,1)S(1)}, u32[]{:S(2)}, u32[]{:S(2)}) collective-permute-start(bf16[32,3072]{1,0:T(8,128)(2,1)S(1)} %slice.67), channel_id=1, source_target_pairs={{0,32},{1,97},{32,64},{33,1},{64,96},{65,33},{96,0},{97,65},{2,34}... | collective-permute-start | bytes 589832 | tf_op jit(solution)/shard_map/ppermute | solution.py:343
  63.6 2.1 %collective-permute-done.19.refs_14_ = bf16[32,3072]{1,0:T(8,128)(2,1)S(1)} collective-permute-done((bf16[32,3072]{1,0:T(8,128)(2,1)S(1)}, bf16[32,3072]{1,0:T(8,128)(2,1)S(1)}, u32[]{:S(2)}, u32[]{:S(2)}) %collective-permute-start.19) | collective-permute-done | bytes 196640 | tf_op jit(solution)/shard_map/ppermute | solution.py:343
  66.2 3.4 %collective-permute-start.22 = (bf16[2,64,3072]{2,1,0:T(8,128)(2,1)S(1)}, bf16[2,64,3072]{2,1,0:T(8,128)(2,1)S(1)}, u32[]{:S(2)}, u32[]{:S(2)}) collective-permute-start(bf16[2,64,3072]{2,1,0:T(8,128)(2,1)S(1)} %collective-permute-done.17.refs_18_), channel_id=1, source_target_pairs={{0,1},{1,0},{2,3},{3,2},{4,5},{5,4},{6,7},{7,6},{8,9},{9,8},{10,11... | collective-permute-start | bytes 2359304 | tf_op jit(solution)/shard_map/ppermute | solution.py:336
  69.6 2.5 %collective-permute-done.23.refs_23_ = bf16[64,3072]{1,0:T(8,128)(2,1)S(1)} collective-permute-done((bf16[64,3072]{1,0:T(8,128)(2,1)S(1)}, bf16[64,3072]{1,0:T(8,128)(2,1)S(1)}, u32[]{:S(2)}, u32[]{:S(2)}) %collective-permute-start.23) | collective-permute-done | bytes 393248 | tf_op jit(solution)/shard_map/ppermute | solution.py:336
  72.1 15.8 %logits.1 = (f32[1024,1024]{1,0:T(8,128)S(1)}, f32[1024,1024]{1,0:T(8,128)S(1)}, f32[2,1024]{1,0:T(2,128)S(1)}, f32[2,1024]{1,0:T(2,128)S(1)}, bf16[1024,512]{1,...) custom-call(bf16[64,3072]{1,0:T(8,128)(2,1)S(1)} %pack_rows.1.refs_0_, bf16[64,3072]{1,0:T(8,128)(2,1)S(1)} %collective-permute-done.refs_1_, ...), custom_call_target="tpu_custom_call" | custom-call | flops 9126805504 | bytes 20971520 | tf_op jit(solution)/shard_map/logits/pallas_call | solution.py:180
  92.0 2.3 %collective-permute-done.25 = f32[2,1024]{1,0:T(2,128)S(1)} collective-permute-done((f32[2,1024]{1,0:T(2,128)S(1)}, f32[2,1024]{1,0:T(2,128)S(1)}, u32[]{:S(2)}, u32[]{:S(2)}) %collective-permute-start.25) | collective-permute-done | bytes 8224 | tf_op jit(solution)/shard_map/ppermute | solution.py:348
  98.8 3.7 %collective-permute-start.31 = (f32[2,1024]{1,0:T(2,128)S(1)}, f32[2,1024]{1,0:T(2,128)S(1)}, u32[]{:S(2)}, u32[]{:S(2)}) collective-permute-start(f32[2,1024]{1,0:T(2,128)S(1)} %multiply_add_fusion.1), channel_id=1, source_target_pairs={{0,128},{2,130},{4,132},{6,134},{128,0},{130,2},{132,4},{134,6},{1... | collective-permute-start | bytes 24584 | tf_op jit(solution)/shard_map/ppermute | solution.py:348
  102.6 2.8 %collective-permute-done.31 = f32[2,1024]{1,0:T(2,128)S(1)} collective-permute-done((f32[2,1024]{1,0:T(2,128)S(1)}, f32[2,1024]{1,0:T(2,128)S(1)}, u32[]{:S(2)}, u32[]{:S(2)}) %collective-permute-start.31) | collective-permute-done | bytes 8224 | tf_op jit(solution)/shard_map/ppermute | solution.py:348
  105.4 4.2 %weights.1 = (bf16[1024,1024]{1,0:T(8,128)(2,1)S(1)}, f32[512,512]{1,0:T(8,128)S(1)}, f32[512,512]{1,0:T(8,128)S(1)}) custom-call(f32[1024,1024]{1,0:T(8,128)S(1)} %get-tuple-element.62.t_ref, f32[1024,1024]{1,0:T(8,128)S(1)} %get-tuple-element.63.s_ref, f32[2,1024]{1,0:T(2,128)S(1)} %multiply_add_fusion.4.row_ref, f32[2,1024]{1,0:T(2,128)S(1)} %multiply_add_fusion.col_ref, ...), custom_call_target="tpu_custom_call" | custom-call | flops 1073741824 | bytes 10485760 | tf_op jit(solution)/shard_map/weights/pallas_call | solution.py:259
  109.6 5.3 %collective-permute-start.32 = (f32[512,512]{1,0:T(8,128)S(1)}, f32[512,512]{1,0:T(8,128)S(1)}, u32[]{:S(2)}, u32[]{:S(2)}) collective-permute-start(f32[512,512]{1,0:T(8,128)S(1)} %get-tuple-element.70), channel_id=1, source_target_pairs={{0,1},{1,0},{2,3},{3,2},{4,5},{5,4},{6,7},{7,6},{8,9},{9,8},{10,11... | collective-permute-start | bytes 3145736 | tf_op jit(solution)/shard_map/ppermute | solution.py:336
  114.9 2.2 %img_terms.1 = bf16[1024,512]{1,0:T(8,128)(2,1)} custom-call(bf16[1024,1024]{1,0:T(8,128)(2,1)S(1)} %get-tuple-element.67.w_ref, bf16[1024,512]{1,0:T(8,128)(2,1)S(1)} %get-tuple-element.68.scol_ref), custom_call_target="tpu_custom_call" | custom-call | flops 1073741824 | bytes 4194304 | tf_op jit(solution)/shard_map/img_terms/pallas_call | solution.py:296
  117.1 4.3 %all-to-all-start = ((bf16[16,64,512]{2,1,0:T(8,128)(2,1)}), bf16[16,64,512]{2,1,0:T(8,128)(2,1)}, u32[]{:S(2)}, u32[]{:S(2)}) async-start(bf16[16,64,512]{2,1,0:T(8,128)(2,1)} %bitcast.5), calls=%async_computation | async-start | bytes 2097152 | tf_op jit(solution)/shard_map/all_to_all | solution.py:409
  121.6 2.7 %collective-permute-start.33 = (bf16[128,512]{1,0:T(8,128)(2,1)S(1)}, bf16[128,512]{1,0:T(8,128)(2,1)S(1)}, u32[]{:S(2)}, u32[]{:S(2)}) collective-permute-start(bf16[128,512]{1,0:T(8,128)(2,1)S(1)} %get-tuple-element.72), channel_id=1, source_target_pairs={{0,2},{1,135},{2,4},{3,1},{4,6},{5,3},{6,128},{7,5},{128,130},{129... | collective-permute-start | bytes 393224 | tf_op jit(solution)/shard_map/ppermute | solution.py:343
  125.0 2.3 %collective-permute-start.35 = (bf16[128,512]{1,0:T(8,128)(2,1)S(1)}, bf16[128,512]{1,0:T(8,128)(2,1)S(1)}, u32[]{:S(2)}, u32[]{:S(2)}) collective-permute-start(bf16[128,512]{1,0:T(8,128)(2,1)S(1)} %get-tuple-element.74), channel_id=1, source_target_pairs={{0,6},{1,131},{2,128},{3,133},{4,130},{5,135},{6,132},{7,1},{128,1... | collective-permute-start | bytes 393224 | tf_op jit(solution)/shard_map/ppermute | solution.py:343
  127.3 3.2 %collective-permute-start.36 = (bf16[64,512]{1,0:T(8,128)(2,1)S(1)}, bf16[64,512]{1,0:T(8,128)(2,1)S(1)}, u32[]{:S(2)}, u32[]{:S(2)}) collective-permute-start(bf16[64,512]{1,0:T(8,128)(2,1)S(1)} %get-tuple-element.75), channel_id=1, source_target_pairs={{0,128},{1,129},{2,130},{3,131},{4,132},{5,133},{6,134},{7,135},{1... | collective-permute-start | bytes 196616 | tf_op jit(solution)/shard_map/ppermute | solution.py:343
  131.8 5.5 %collective-permute-start.37 = (f32[64,512]{1,0:T(8,128)S(1)}, f32[64,512]{1,0:T(8,128)S(1)}, u32[]{:S(2)}, u32[]{:S(2)}) collective-permute-start(f32[64,512]{1,0:T(8,128)S(1)} %slice_add_fusion), channel_id=1, source_target_pairs={{0,1},{1,0},{2,3},{3,2},{4,5},{5,4},{6,7},{7,6},{8,9},{9,8},{10,11... | collective-permute-start | bytes 393224 | tf_op jit(solution)/shard_map/ppermute | solution.py:336
  (100 shorter events, 34.0 us)
Async XLA Ops:
  7.4 19.1 %collective-permute-start.6 = (bf16[2,64,3072]{2,1,0:T(8,128)(2,1)S(1)}, bf16[2,64,3072]{2,1,0:T(8,128)(2,1)S(1)}, u32[]{:S(2)}, u32[]{:S(2)}) collective-permute-start(bf16[2,64,3072]{2,1,0:T(8,128)(2,1)S(1)} %pack_cols.1.refs_15_), channel_id=1, source_target_pairs={{0,2},{1,135},{2,4},{3,1},{4,6},{5,3},{6,128},{7,5},{128,130},{129... | collective-permute-start | bytes 2359304 | tf_op jit(solution)/shard_map/ppermute | solution.py:343
  11.4 12.4 %collective-permute-start.3 = (bf16[64,3072]{1,0:T(8,128)(2,1)S(1)}, bf16[64,3072]{1,0:T(8,128)(2,1)S(1)}, u32[]{:S(2)}, u32[]{:S(2)}) collective-permute-start(bf16[64,3072]{1,0:T(8,128)(2,1)S(1)} %pack_rows.1.refs_0_), channel_id=1, source_target_pairs={{0,24},{1,9},{8,0},{9,17},{16,8},{17,25},{24,16},{25,1},{2,26},{3,... | collective-permute-start | bytes 1179656 | tf_op jit(solution)/shard_map/ppermute | solution.py:343
  12.8 11.0 %collective-permute-start.2 = (bf16[64,3072]{1,0:T(8,128)(2,1)S(1)}, bf16[64,3072]{1,0:T(8,128)(2,1)S(1)}, u32[]{:S(2)}, u32[]{:S(2)}) collective-permute-start(bf16[64,3072]{1,0:T(8,128)(2,1)S(1)} %pack_rows.1.refs_0_), channel_id=1, source_target_pairs={{0,8},{1,25},{8,16},{9,1},{16,24},{17,9},{24,0},{25,17},{2,10},{3,... | collective-permute-start | bytes 1179656 | tf_op jit(solution)/shard_map/ppermute | solution.py:343
  14.3 12.2 %collective-permute-start.1 = (bf16[64,3072]{1,0:T(8,128)(2,1)S(1)}, bf16[64,3072]{1,0:T(8,128)(2,1)S(1)}, u32[]{:S(2)}, u32[]{:S(2)}) collective-permute-start(bf16[64,3072]{1,0:T(8,128)(2,1)S(1)} %pack_rows.1.refs_0_), channel_id=1, source_target_pairs={{0,96},{1,33},{32,0},{33,65},{64,32},{65,97},{96,64},{97,1},{2,98}... | collective-permute-start | bytes 1179656 | tf_op jit(solution)/shard_map/ppermute | solution.py:343
  15.5 11.0 %collective-permute-start = (bf16[64,3072]{1,0:T(8,128)(2,1)S(1)}, bf16[64,3072]{1,0:T(8,128)(2,1)S(1)}, u32[]{:S(2)}, u32[]{:S(2)}) collective-permute-start(bf16[64,3072]{1,0:T(8,128)(2,1)S(1)} %pack_rows.1.refs_0_), channel_id=1, source_target_pairs={{0,32},{1,97},{32,64},{33,1},{64,96},{65,33},{96,0},{97,65},{2,34}... | collective-permute-start | bytes 1179656 | tf_op jit(solution)/shard_map/ppermute | solution.py:343
  27.2 17.3 %collective-permute-start.9 = (bf16[128,3072]{1,0:T(8,128)(2,1)S(1)}, bf16[128,3072]{1,0:T(8,128)(2,1)S(1)}, u32[]{:S(2)}, u32[]{:S(2)}) collective-permute-start(bf16[128,3072]{1,0:T(8,128)(2,1)S(1)} %pad_maximum_fusion.1), channel_id=1, source_target_pairs={{0,8},{1,25},{8,16},{9,1},{16,24},{17,9},{24,0},{25,17},{2,10},{3,... | collective-permute-start | bytes 2359304 | tf_op jit(solution)/shard_map/ppermute | solution.py:343
  28.7 15.8 %collective-permute-start.7 = (bf16[128,3072]{1,0:T(8,128)(2,1)S(1)}, bf16[128,3072]{1,0:T(8,128)(2,1)S(1)}, u32[]{:S(2)}, u32[]{:S(2)}) collective-permute-start(bf16[128,3072]{1,0:T(8,128)(2,1)S(1)} %pad_maximum_fusion), channel_id=1, source_target_pairs={{0,32},{1,97},{32,64},{33,1},{64,96},{65,33},{96,0},{97,65},{2,34}... | collective-permute-start | bytes 2359304 | tf_op jit(solution)/shard_map/ppermute | solution.py:343
  29.6 14.9 %collective-permute-start.12 = (bf16[2,64,3072]{2,1,0:T(8,128)(2,1)S(1)}, bf16[2,64,3072]{2,1,0:T(8,128)(2,1)S(1)}, u32[]{:S(2)}, u32[]{:S(2)}) collective-permute-start(bf16[2,64,3072]{2,1,0:T(8,128)(2,1)S(1)} %collective-permute-done.6.refs_16_), channel_id=1, source_target_pairs={{0,2},{1,135},{2,4},{3,1},{4,6},{5,3},{6,128},{7,5},{128,130},{129... | collective-permute-start | bytes 2359304 | tf_op jit(solution)/shard_map/ppermute | solution.py:343
  32.3 12.0 %collective-permute-start.10 = (bf16[64,3072]{1,0:T(8,128)(2,1)S(1)}, bf16[64,3072]{1,0:T(8,128)(2,1)S(1)}, u32[]{:S(2)}, u32[]{:S(2)}) collective-permute-start(bf16[64,3072]{1,0:T(8,128)(2,1)S(1)} %pad_maximum_fusion.5), channel_id=1, source_target_pairs={{0,24},{1,9},{8,0},{9,17},{16,8},{17,25},{24,16},{25,1},{2,26},{3,... | collective-permute-start | bytes 1179656 | tf_op jit(solution)/shard_map/ppermute | solution.py:343
  32.5 12.0 %collective-permute-start.8 = (bf16[64,3072]{1,0:T(8,128)(2,1)S(1)}, bf16[64,3072]{1,0:T(8,128)(2,1)S(1)}, u32[]{:S(2)}, u32[]{:S(2)}) collective-permute-start(bf16[64,3072]{1,0:T(8,128)(2,1)S(1)} %pad_maximum_fusion.4), channel_id=1, source_target_pairs={{0,96},{1,33},{32,0},{33,65},{64,32},{65,97},{96,64},{97,1},{2,98}... | collective-permute-start | bytes 1179656 | tf_op jit(solution)/shard_map/ppermute | solution.py:343
  44.7 13.3 %collective-permute-start.15 = (bf16[96,3072]{1,0:T(8,128)(2,1)S(1)}, bf16[96,3072]{1,0:T(8,128)(2,1)S(1)}, u32[]{:S(2)}, u32[]{:S(2)}) collective-permute-start(bf16[96,3072]{1,0:T(8,128)(2,1)S(1)} %pad_maximum_fusion.3), channel_id=1, source_target_pairs={{0,8},{1,25},{8,16},{9,1},{16,24},{17,9},{24,0},{25,17},{2,10},{3,... | collective-permute-start | bytes 1769480 | tf_op jit(solution)/shard_map/ppermute | solution.py:343
  47.6 11.3 %collective-permute-start.17 = (bf16[2,64,3072]{2,1,0:T(8,128)(2,1)S(1)}, bf16[2,64,3072]{2,1,0:T(8,128)(2,1)S(1)}, u32[]{:S(2)}, u32[]{:S(2)}) collective-permute-start(bf16[2,64,3072]{2,1,0:T(8,128)(2,1)S(1)} %collective-permute-done.12.refs_17_), channel_id=1, source_target_pairs={{0,2},{1,135},{2,4},{3,1},{4,6},{5,3},{6,128},{7,5},{128,130},{129... | collective-permute-start | bytes 2359304 | tf_op jit(solution)/shard_map/ppermute | solution.py:343
  48.4 10.5 %collective-permute-start.13 = (bf16[96,3072]{1,0:T(8,128)(2,1)S(1)}, bf16[96,3072]{1,0:T(8,128)(2,1)S(1)}, u32[]{:S(2)}, u32[]{:S(2)}) collective-permute-start(bf16[96,3072]{1,0:T(8,128)(2,1)S(1)} %pad_maximum_fusion.2), channel_id=1, source_target_pairs={{0,32},{1,97},{32,64},{33,1},{64,96},{65,33},{96,0},{97,65},{2,34}... | collective-permute-start | bytes 1769480 | tf_op jit(solution)/shard_map/ppermute | solution.py:343
  49.2 8.2 %collective-permute-start.14 = (bf16[32,3072]{1,0:T(8,128)(2,1)S(1)}, bf16[32,3072]{1,0:T(8,128)(2,1)S(1)}, u32[]{:S(2)}, u32[]{:S(2)}) collective-permute-start(bf16[32,3072]{1,0:T(8,128)(2,1)S(1)} %slice.64), channel_id=1, source_target_pairs={{0,96},{1,33},{32,0},{33,65},{64,32},{65,97},{96,64},{97,1},{2,98}... | collective-permute-start | bytes 589832 | tf_op jit(solution)/shard_map/ppermute | solution.py:343
  50.1 7.8 %collective-permute-start.16 = (bf16[32,3072]{1,0:T(8,128)(2,1)S(1)}, bf16[32,3072]{1,0:T(8,128)(2,1)S(1)}, u32[]{:S(2)}, u32[]{:S(2)}) collective-permute-start(bf16[32,3072]{1,0:T(8,128)(2,1)S(1)} %slice.66), channel_id=1, source_target_pairs={{0,24},{1,9},{8,0},{9,17},{16,8},{17,25},{24,16},{25,1},{2,26},{3,... | collective-permute-start | bytes 589832 | tf_op jit(solution)/shard_map/ppermute | solution.py:343
  58.9 7.3 %collective-permute-start.20 = (bf16[64,3072]{1,0:T(8,128)(2,1)S(1)}, bf16[64,3072]{1,0:T(8,128)(2,1)S(1)}, u32[]{:S(2)}, u32[]{:S(2)}) collective-permute-start(bf16[64,3072]{1,0:T(8,128)(2,1)S(1)} %slice_bitcast_fusion), channel_id=1, source_target_pairs={{0,2},{1,135},{2,4},{3,1},{4,6},{5,3},{6,128},{7,5},{128,130},{129... | collective-permute-start | bytes 1179656 | tf_op jit(solution)/shard_map/ppermute | solution.py:343
  98.8 6.5 %collective-permute-start.31 = (f32[2,1024]{1,0:T(2,128)S(1)}, f32[2,1024]{1,0:T(2,128)S(1)}, u32[]{:S(2)}, u32[]{:S(2)}) collective-permute-start(f32[2,1024]{1,0:T(2,128)S(1)} %multiply_add_fusion.1), channel_id=1, source_target_pairs={{0,128},{2,130},{4,132},{6,134},{128,0},{130,2},{132,4},{134,6},{1... | collective-permute-start | bytes 24584 | tf_op jit(solution)/shard_map/ppermute | solution.py:348
  109.6 11.9 %collective-permute-start.32 = (f32[512,512]{1,0:T(8,128)S(1)}, f32[512,512]{1,0:T(8,128)S(1)}, u32[]{:S(2)}, u32[]{:S(2)}) collective-permute-start(f32[512,512]{1,0:T(8,128)S(1)} %get-tuple-element.70), channel_id=1, source_target_pairs={{0,1},{1,0},{2,3},{3,2},{4,5},{5,4},{6,7},{7,6},{8,9},{9,8},{10,11... | collective-permute-start | bytes 3145736 | tf_op jit(solution)/shard_map/ppermute | solution.py:336
  117.1 21.5 %all-to-all-start = ((bf16[16,64,512]{2,1,0:T(8,128)(2,1)}), bf16[16,64,512]{2,1,0:T(8,128)(2,1)}, u32[]{:S(2)}, u32[]{:S(2)}) async-start(bf16[16,64,512]{2,1,0:T(8,128)(2,1)} %bitcast.5), calls=%async_computation | async-start | bytes 2097152 | tf_op jit(solution)/shard_map/all_to_all | solution.py:409
  121.6 8.9 %collective-permute-start.33 = (bf16[128,512]{1,0:T(8,128)(2,1)S(1)}, bf16[128,512]{1,0:T(8,128)(2,1)S(1)}, u32[]{:S(2)}, u32[]{:S(2)}) collective-permute-start(bf16[128,512]{1,0:T(8,128)(2,1)S(1)} %get-tuple-element.72), channel_id=1, source_target_pairs={{0,2},{1,135},{2,4},{3,1},{4,6},{5,3},{6,128},{7,5},{128,130},{129... | collective-permute-start | bytes 393224 | tf_op jit(solution)/shard_map/ppermute | solution.py:343
  124.2 7.4 %collective-permute-start.34 = (bf16[128,512]{1,0:T(8,128)(2,1)S(1)}, bf16[128,512]{1,0:T(8,128)(2,1)S(1)}, u32[]{:S(2)}, u32[]{:S(2)}) collective-permute-start(bf16[128,512]{1,0:T(8,128)(2,1)S(1)} %get-tuple-element.73), channel_id=1, source_target_pairs={{0,4},{1,133},{2,6},{3,135},{4,128},{5,1},{6,130},{7,3},{128,132},... | collective-permute-start | bytes 393224 | tf_op jit(solution)/shard_map/ppermute | solution.py:343
  125.0 6.7 %collective-permute-start.35 = (bf16[128,512]{1,0:T(8,128)(2,1)S(1)}, bf16[128,512]{1,0:T(8,128)(2,1)S(1)}, u32[]{:S(2)}, u32[]{:S(2)}) collective-permute-start(bf16[128,512]{1,0:T(8,128)(2,1)S(1)} %get-tuple-element.74), channel_id=1, source_target_pairs={{0,6},{1,131},{2,128},{3,133},{4,130},{5,135},{6,132},{7,1},{128,1... | collective-permute-start | bytes 393224 | tf_op jit(solution)/shard_map/ppermute | solution.py:343
  127.3 13.4 %collective-permute-start.36 = (bf16[64,512]{1,0:T(8,128)(2,1)S(1)}, bf16[64,512]{1,0:T(8,128)(2,1)S(1)}, u32[]{:S(2)}, u32[]{:S(2)}) collective-permute-start(bf16[64,512]{1,0:T(8,128)(2,1)S(1)} %get-tuple-element.75), channel_id=1, source_target_pairs={{0,128},{1,129},{2,130},{3,131},{4,132},{5,133},{6,134},{7,135},{1... | collective-permute-start | bytes 196616 | tf_op jit(solution)/shard_map/ppermute | solution.py:343
  131.8 8.9 %collective-permute-start.37 = (f32[64,512]{1,0:T(8,128)S(1)}, f32[64,512]{1,0:T(8,128)S(1)}, u32[]{:S(2)}, u32[]{:S(2)}) collective-permute-start(f32[64,512]{1,0:T(8,128)S(1)} %slice_add_fusion), channel_id=1, source_target_pairs={{0,1},{1,0},{2,3},{3,2},{4,5},{5,4},{6,7},{7,6},{8,9},{9,8},{10,11... | collective-permute-start | bytes 393224 | tf_op jit(solution)/shard_map/ppermute | solution.py:336
  (19 other events, 76.0 us)
where the time goes:
time: 142 us; the launch traced here: 141 us
  starting transfers between devices  65.3 us (46%)
  waiting for transfers between devices  47.4 us (33%)
  Pallas kernels  22.5 us (16%)
  other arithmetic  3.29 us (2%)
  local copies, waits for them, and re-layouts  2.02 us (1%)
    ppermute x22, waiting for transfers between devices, turn(): return lax.ppermute(x, axes, pairs)  34 us
    ppermute x22, starting transfers between devices, turn(): return lax.ppermute(x, axes, pairs)  33.6 us
    ppermute x9, starting transfers between devices, swap(): return lax.ppermute(x, 'core', [(0, 1), (1, 0)])  18.6 us
    pallas_call x1, Pallas kernels, logits(): pl.pallas_call(kernel, in_specs=[VMEM] * (n_rows + n_cols), out_specs=[VM...  15.8 us
    ppermute x7, starting transfers between devices, join_along(): return join(x, lax.ppermute(x, axis, [(i, i ^ step) for i in range(n)]))  8.77 us
    ppermute x7, waiting for transfers between devices, join_along(): return join(x, lax.ppermute(x, axis, [(i, i ^ step) for i in range(n)]))  7.97 us
    all_to_all x1, starting transfers between devices, local(): lax.all_to_all(img_terms(w, scol).reshape(-1, share, ds), PLANE, 0, 0)  4.33 us
    pallas_call x1, Pallas kernels, weights(): pl.pallas_call(kernel, grid=(m // block,), in_specs=[pl.BlockSpec((block,...  4.21 us
  transfers between devices with their start and end apart: 39, of which 18 were waited for; matrix products, arithmetic and copies ran while one was open for 2% of the time, Pallas kernels for 2%

commit v1 on v0

--- a/solution.py
+++ b/solution.py
@@ -46,29 +46,46 @@
     out_ref[:, 2 * width :] = s
 
 
-def pack_rows(t, s):
-    def kernel(t_ref, s_ref, out_ref):
-        split(t_ref[...], s_ref[...], out_ref, ("high", "low"))
-
-    return pl.pallas_call(
-        kernel,
-        out_shape=jax.ShapeDtypeStruct((t.shape[0], 2 * t.shape[1] + s.shape[1]), BF16),
+def pack(*shards):
+    share, width = shards[0].shape
+    total = 2 * width + shards[1].shape[1]
+
+    def kernel(*refs):
+        sources, (rows_ref, cols_ref), (*bufs, sem) = refs[:4], refs[4:6], refs[6:]
+        copies = [
+            pltpu.make_async_copy(src, buf, sem.at[i])
+            for i, (src, buf) in enumerate(zip(sources, bufs))
+        ]
+        for copy in copies:
+            copy.start()
+        for copy in copies:
+            copy.wait()
+        split(bufs[0][...], bufs[1][...], rows_ref, ("high", "low"))
+        split(bufs[2][...], bufs[3][...], cols_ref, ("low", "high"))
+
+    return pl.pallas_call(
+        kernel,
+        in_specs=[pl.BlockSpec(memory_space=pltpu.HBM)] * 4,
+        out_specs=[VMEM] * 2,
+        out_shape=[jax.ShapeDtypeStruct((share, total), BF16)] * 2,
+        scratch_shapes=[pltpu.VMEM(v.shape, v.dtype) for v in shards]
+        + [pltpu.SemaphoreType.DMA((4,))],
+        compiler_params=pltpu.CompilerParams(vmem_limit_bytes=63 * MIB),
+        name="pack",
+    )(*shards)
+
+
+def pair(cols, t_other, s_other):
+    def kernel(cols_ref, t_ref, s_ref, out_ref):
+        out_ref[0] = cols_ref[...]
+        split(t_ref[...], s_ref[...], out_ref.at[1], ("low", "high"))
+
+    return pl.pallas_call(
+        kernel,
+        out_shape=jax.ShapeDtypeStruct((2,) + cols.shape, BF16),
         compiler_params=pltpu.CompilerParams(vmem_limit_bytes=16 * MIB),
-        name="pack_rows",
-    )(t, s)
-
-
-def pack_cols(t, s, t_other, s_other):
-    def kernel(t_ref, s_ref, t_other_ref, s_other_ref, out_ref):
-        split(t_ref[...], s_ref[...], out_ref.at[0], ("low", "high"))
-        split(t_other_ref[...], s_other_ref[...], out_ref.at[1], ("low", "high"))
-
-    return pl.pallas_call(
-        kernel,
-        out_shape=jax.ShapeDtypeStruct((2, t.shape[0], 2 * t.shape[1] + s.shape[1]), BF16),
-        compiler_params=pltpu.CompilerParams(vmem_limit_bytes=16 * MIB),
-        name="pack_cols",
-    )(t, s, t_other, s_other)
+        name="pair",
+    )(cols, t_other, s_other)
 
 
 def row_plan(x, y, sign, share):
@@ -139,11 +156,11 @@
 
         def place(src, first, buf, at, size):
             def some_rows(i, _):
-                there = pl.ds(pl.multiple_of(at + 16 * i, 16), 16)
-                buf[there, :] = src[pl.ds(pl.multiple_of(first + 16 * i, 16), 16), :]
+                there = pl.ds(pl.multiple_of(at + 32 * i, 32), 32)
+                buf[there, :] = src[pl.ds(pl.multiple_of(first + 32 * i, 32), 32), :]
                 return 0
 
-            lax.fori_loop(0, size // 16, some_rows, 0)
+            lax.fori_loop(0, size // 32, some_rows, 0)
 
         for piece, first, size, at in row_plan(x, y, sign, share):
             place(rows_in[piece], first, r_buf, at, size)
@@ -203,13 +220,13 @@
     )(*row_pieces, *col_pieces)
 
 
-def weights(t, s, row_lse, col_lse, srow, share, ring):
+def weights(t, s, row_lse, col_lse, srow, scol, share, ring):
     m, n = t.shape
     ds = srow.shape[1]
     block = 512
 
     def kernel(
-        t_ref, s_ref, row_ref, col_ref, srow_ref, w_ref, mine_ref, theirs_ref, lse, acc
+        t_ref, s_ref, row_ref, col_ref, srow_ref, scol_ref, img_ref, mine_ref, theirs_ref, lse, acc
     ):
         step = pl.program_id(0)
 
@@ -225,8 +242,8 @@
         along_rows = jnp.exp2(s - row[:, 1:2]) - jnp.exp2(t - row[:, 0:1])
         along_cols = jnp.exp2(s - col_ref[1:2, :]) - jnp.exp2(t - col_ref[0:1, :])
         w = (weight_scale * (along_rows + along_cols)).astype(BF16)
-        w_ref[...] = w
         part = tn(w, srow_ref[...])
+        img_ref[...] = jnp.dot(w, scol_ref[...], preferred_element_type=F32).astype(BF16)
 
         @pl.when(step == 0)
         def _():
@@ -265,49 +282,37 @@
             pl.BlockSpec((2, m), lambda i: (0, 0)),
             pl.BlockSpec((2, n), lambda i: (0, 0)),
             pl.BlockSpec((block, ds), lambda i: (i, 0)),
+            pl.BlockSpec((n, ds), lambda i: (0, 0)),
         ],
         out_specs=[
-            pl.BlockSpec((block, n), lambda i: (i, 0)),
+            pl.BlockSpec((block, ds), lambda i: (i, 0)),
             pl.BlockSpec((n // 2, ds), lambda i: (0, 0)),
             pl.BlockSpec((n // 2, ds), lambda i: (0, 0)),
         ],
         out_shape=[
-            jax.ShapeDtypeStruct((m, n), BF16),
+            jax.ShapeDtypeStruct((m, ds), BF16),
             jax.ShapeDtypeStruct((n // 2, ds), F32),
             jax.ShapeDtypeStruct((n // 2, ds), F32),
         ],
         scratch_shapes=[pltpu.VMEM((m, 128), F32), pltpu.VMEM((n, ds), F32)],
         compiler_params=pltpu.CompilerParams(vmem_limit_bytes=20 * MIB),
         cost_estimate=pl.CostEstimate(
-            flops=2 * m * n * ds, bytes_accessed=10 * m * n, transcendentals=4 * m * n
+            flops=4 * m * n * ds, bytes_accessed=10 * m * n, transcendentals=4 * m * n
         ),
         name="weights",
-    )(t, s, row_lse, col_lse, srow)
-
-
-def img_terms(w, scol):
-    m, n = w.shape
-    ds = scol.shape[1]
-    block = 512
-
-    def kernel(w_ref, scol_ref, img_ref):
-        img_ref[...] = jnp.dot(w_ref[...], scol_ref[...], preferred_element_type=F32).astype(BF16)
-
-    return pl.pallas_call(
-        kernel,
-        grid=(m // block,),
-        in_specs=[
-            pl.BlockSpec((block, n), lambda i: (i, 0)),
-            pl.BlockSpec((n, ds), lambda i: (0, 0)),
-        ],
-        out_specs=pl.BlockSpec((block, ds), lambda i: (i, 0)),
-        out_shape=jax.ShapeDtypeStruct((m, ds), BF16),
+    )(t, s, row_lse, col_lse, srow, scol)
+
+
+def add_up(terms):
+    def kernel(terms_ref, out_ref):
+        out_ref[...] = jnp.sum(terms_ref[...].astype(F32), axis=0)
+
+    return pl.pallas_call(
+        kernel,
+        out_shape=jax.ShapeDtypeStruct(terms.shape[1:], F32),
         compiler_params=pltpu.CompilerParams(vmem_limit_bytes=10 * MIB),
-        cost_estimate=pl.CostEstimate(
-            flops=2 * m * n * ds, bytes_accessed=4 * m * n, transcendentals=0
-        ),
-        name="img_terms",
-    )(w, scol)
+        name="add_up",
+    )(terms)
 
 
 def deal(mine, came, share, ring):
@@ -379,44 +384,48 @@
             turn(c2, RING, 1),
         )
     )
-    x4, y4, c4, d2, c3 = hold(
-        (turn(x3[share:], "x", 1), turn(y3[share:], "y", 1), turn(c3[0], RING, 1), swap(c2), c3)
+    x4, y4, c4, d2, d3 = hold(
+        (
+            turn(x3[share:], "x", 1),
+            turn(y3[share:], "y", 1),
+            turn(c3[0], RING, 1),
+            swap(c2),
+            swap(c3),
+        )
     )
     rows = [r, x1, x1r, y1, y1r, x2, x2r, y2, y2r, x3, x3r, y3, y3r, x4, y4]
-    return rows, [c0, c1, c2, c3, d1, d2, swap(c3), c4, swap(c4)]
+    return rows, [c0, c1, c2, c3, d1, d2, d3, c4, swap(c4)]
 
 
 def local(teacher_img, teacher_cap, student_img, student_cap):
     width = teacher_img.shape[3]
     share, ds = student_img.shape[2:]
     ring = lax.axis_size(RING)
-    rows_own = pack_rows(teacher_img[0, 0], student_img[0, 0])
-    cols_own = (teacher_cap[0, 0], student_cap[0, 0])
-    cols_pair = pack_cols(*cols_own, *[swap(v) for v in cols_own])
+    came = swap(teacher_cap[0, 0]), swap(student_cap[0, 0])
+    rows_own, cols_own = pack(
+        teacher_img[0, 0], student_img[0, 0], teacher_cap[0, 0], student_cap[0, 0]
+    )
+    cols_pair = pair(cols_own, *came)
     rows, cols = gather(rows_own, cols_pair, share)
     t, s, row_lse, col_lse, srow, scol = logits(rows, cols, width, share, ring)
 
     came = swap(col_lse)
     half = ring * share
     col_lse = join(col_lse, jnp.concatenate([came[:, half:], came[:, :half]], axis=1))
-    for step in (1, 2, 4):
+    for step in (1, 2, 7):
         col_lse = join_along(col_lse, RING, step)
     for axis in PLANE:
         for step in (1, 3):
             row_lse = join_along(row_lse, axis, step)
 
-    w, mine, theirs = weights(t, s, row_lse, col_lse, srow, share, ring)
-    img_sent = lax.all_to_all(img_terms(w, scol).reshape(-1, share, ds), PLANE, 0, 0)
+    img, mine, theirs = weights(t, s, row_lse, col_lse, srow, scol, share, ring)
+    img_sent = lax.all_to_all(img.reshape(-1, share, ds), PLANE, 0, 0)
     *dealt, own = deal(mine, swap(theirs), share, ring)
-    other = None
-    for k, terms in enumerate(dealt, 1):
-        terms = turn(terms, RING, k).astype(F32)
-        own = own + terms[:share]
-        if terms.shape[0] > share:
-            other = terms[share:] if other is None else other + terms[share:]
-    grad_cap = own + swap(other)
-    grad_img = jnp.sum(img_sent.astype(F32), axis=0)
-    return grad_img[None, None], grad_cap[None, None]
+    dealt = lax.optimization_barrier([turn(v, RING, k) for k, v in enumerate(dealt, 1)])
+    *both, far = [v.astype(F32) for v in dealt]
+    other = sum(v[share:] for v in both[1:]) + both[0][share:]
+    grad_cap = own + far + sum(v[:share] for v in both[1:]) + both[0][:share] + swap(other)
+    return add_up(img_sent)[None, None], grad_cap[None, None]
 
 
 def solution(mesh):

time: 142 us -> 138 us (0.972)
  starting transfers between devices: 65.3 us -> 61.8 us
  Pallas kernels: 22.5 us -> 24.9 us
  other arithmetic: 3.29 us -> 1.26 us
    ppermute x22, waiting for transfers between devices: 34 us -> 38.2 us  [turn(): return lax.ppermute(x, axes, pairs)]
    ppermute x9, waiting for transfers between devices: 3.95 us -> 1.56 us  [swap(): return lax.ppermute(x, 'core', [(0, 1), (1, 0)])]
    pallas_call x1, Pallas kernels: 4.21 us -> 6.51 us  [weights(): pl.pallas_call(kernel, grid=(m // block,), in_specs=[pl.BlockSpec((block,...]
    ppermute x7, starting transfers between devices: 8.77 us -> 6.49 us  [join_along(): return join(x, lax.ppermute(x, axis, [(i, i ^ step) for i in range(n)]))]
    reduce_sum x1 -> x0, other arithmetic: 2.03 us -> none  [local(): grad_img = jnp.sum(img_sent.astype(F32), axis=0)]
    ppermute x9, starting transfers between devices: 18.6 us -> 16.8 us  [swap(): return lax.ppermute(x, 'core', [(0, 1), (1, 0)])]
  transfers between devices with their start and end apart: 39 -> 39, of which waited for: 18 -> 17; matrix products, arithmetic and copies ran while one was open for 2% -> 0% of each run, Pallas kernels for 2% -> 2%
where the time goes in v1:
time: 138 us; the launch traced here: 137 us
  starting transfers between devices  61.8 us (45%)
  waiting for transfers between devices  47.3 us (34%)
  Pallas kernels  24.9 us (18%)
    ppermute x22, waiting for transfers between devices, turn(): return lax.ppermute(x, axes, pairs)  38.2 us
    ppermute x22, starting transfers between devices, turn(): return lax.ppermute(x, axes, pairs)  34.6 us
    ppermute x9, starting transfers between devices, swap(): return lax.ppermute(x, 'core', [(0, 1), (1, 0)])  16.8 us
    pallas_call x1, Pallas kernels, logits(): pl.pallas_call(kernel, in_specs=[VMEM] * (n_rows + n_cols), out_specs=[VM...  15.4 us
    ppermute x7, waiting for transfers between devices, join_along(): return join(x, lax.ppermute(x, axis, [(i, i ^ step) for i in range(n)]))  7.54 us
    pallas_call x1, Pallas kernels, weights(): pl.pallas_call(kernel, grid=(m // block,), in_specs=[pl.BlockSpec((block,...  6.51 us
    ppermute x7, starting transfers between devices, join_along(): return join(x, lax.ppermute(x, axis, [(i, i ^ step) for i in range(n)]))  6.49 us
    all_to_all x1, starting transfers between devices, local(): img_sent = lax.all_to_all(img.reshape(-1, share, ds), PLANE, 0, 0)  3.93 us
  transfers between devices with their start and end apart: 39, of which 17 were waited for; matrix products, arithmetic and copies ran while one was open for 0% of the time, Pallas kernels for 2%

profile of v1, /device:TPU:1, one launch (start us, length us, event | category | flops | bytes accessed | tf_op | source)
XLA Modules:
  0.0 137.5 jit_solution(15530014703218297073)
XLA Ops:
  0.6 3.3 %collective-permute-start.4 = (f32[64,1280]{1,0:T(8,128)}, f32[64,1280]{1,0:T(8,128)S(1)}, u32[]{:S(2)}, u32[]{:S(2)}) collective-permute-start(f32[64,1280]{1,0:T(8,128)} %bitcast.11), channel_id=1, source_target_pairs={{0,1},{1,0},{2,3},{3,2},{4,5},{5,4},{6,7},{7,6},{8,9},{9,8},{10,11... | collective-permute-start | bytes 983048 | tf_op jit(solution)/shard_map/ppermute | solution.py:341
  4.1 2.1 %pack.1 = (bf16[64,3072]{1,0:T(8,128)(2,1)}, bf16[64,3072]{1,0:T(8,128)(2,1)}) custom-call(f32[64,1280]{1,0:T(8,128)} %bitcast.10, bf16[64,512]{1,0:T(8,128)(2,1)} %bitcast.14, f32[64,1280]{1,0:T(8,128)} %bitcast.12, bf16[64,512]{1,0:T(8,128)(2,1)} %bitcast.16), custom_call_target="tpu_custom_call" | custom-call | tf_op jit(solution)/shard_map/pack/pallas_call | solution.py:66
  7.2 3.9 %collective-permute-start.6 = (bf16[2,64,3072]{2,1,0:T(8,128)(2,1)S(1)}, bf16[2,64,3072]{2,1,0:T(8,128)(2,1)S(1)}, u32[]{:S(2)}, u32[]{:S(2)}) collective-permute-start(bf16[2,64,3072]{2,1,0:T(8,128)(2,1)S(1)} %pair.1.refs_15_), channel_id=1, source_target_pairs={{0,2},{1,135},{2,4},{3,1},{4,6},{5,3},{6,128},{7,5},{128,130},{129... | collective-permute-start | bytes 2359304 | tf_op jit(solution)/shard_map/ppermute | solution.py:348
  16.6 6.8 %collective-permute-done.3.refs_4_ = bf16[64,3072]{1,0:T(8,128)(2,1)S(1)} collective-permute-done((bf16[64,3072]{1,0:T(8,128)(2,1)S(1)}, bf16[64,3072]{1,0:T(8,128)(2,1)S(1)}, u32[]{:S(2)}, u32[]{:S(2)}) %collective-permute-start.3) | collective-permute-done | bytes 393248 | tf_op jit(solution)/shard_map/ppermute | solution.py:348
  23.4 2.6 %collective-permute-done.1.refs_2_ = bf16[64,3072]{1,0:T(8,128)(2,1)S(1)} collective-permute-done((bf16[64,3072]{1,0:T(8,128)(2,1)S(1)}, bf16[64,3072]{1,0:T(8,128)(2,1)S(1)}, u32[]{:S(2)}, u32[]{:S(2)}) %collective-permute-start.1) | collective-permute-done | bytes 393248 | tf_op jit(solution)/shard_map/ppermute | solution.py:348
  29.4 2.6 %collective-permute-start.12 = (bf16[2,64,3072]{2,1,0:T(8,128)(2,1)S(1)}, bf16[2,64,3072]{2,1,0:T(8,128)(2,1)S(1)}, u32[]{:S(2)}, u32[]{:S(2)}) collective-permute-start(bf16[2,64,3072]{2,1,0:T(8,128)(2,1)S(1)} %collective-permute-done.6.refs_16_), channel_id=1, source_target_pairs={{0,2},{1,135},{2,4},{3,1},{4,6},{5,3},{6,128},{7,5},{128,130},{129... | collective-permute-start | bytes 2359304 | tf_op jit(solution)/shard_map/ppermute | solution.py:348
  32.2 11.7 %collective-permute-done.10.refs_8_ = bf16[64,3072]{1,0:T(8,128)(2,1)S(1)} collective-permute-done((bf16[64,3072]{1,0:T(8,128)(2,1)S(1)}, bf16[64,3072]{1,0:T(8,128)(2,1)S(1)}, u32[]{:S(2)}, u32[]{:S(2)}) %collective-permute-start.10) | collective-permute-done | bytes 393248 | tf_op jit(solution)/shard_map/ppermute | solution.py:348
  44.2 2.8 %collective-permute-start.15 = (bf16[96,3072]{1,0:T(8,128)(2,1)S(1)}, bf16[96,3072]{1,0:T(8,128)(2,1)S(1)}, u32[]{:S(2)}, u32[]{:S(2)}) collective-permute-start(bf16[96,3072]{1,0:T(8,128)(2,1)S(1)} %pad_maximum_fusion.3), channel_id=1, source_target_pairs={{0,8},{1,25},{8,16},{9,1},{16,24},{17,9},{24,0},{25,17},{2,10},{3,... | collective-permute-start | bytes 1769480 | tf_op jit(solution)/shard_map/ppermute | solution.py:348
  49.9 7.4 %collective-permute-done.14.refs_10_ = bf16[32,3072]{1,0:T(8,128)(2,1)S(1)} collective-permute-done((bf16[32,3072]{1,0:T(8,128)(2,1)S(1)}, bf16[32,3072]{1,0:T(8,128)(2,1)S(1)}, u32[]{:S(2)}, u32[]{:S(2)}) %collective-permute-start.14) | collective-permute-done | bytes 196640 | tf_op jit(solution)/shard_map/ppermute | solution.py:348
  60.1 2.5 %collective-permute-start.20 = (bf16[64,3072]{1,0:T(8,128)(2,1)S(1)}, bf16[64,3072]{1,0:T(8,128)(2,1)S(1)}, u32[]{:S(2)}, u32[]{:S(2)}) collective-permute-start(bf16[64,3072]{1,0:T(8,128)(2,1)S(1)} %slice_bitcast_fusion), channel_id=1, source_target_pairs={{0,2},{1,135},{2,4},{3,1},{4,6},{5,3},{6,128},{7,5},{128,130},{129... | collective-permute-start | bytes 1179656 | tf_op jit(solution)/shard_map/ppermute | solution.py:348
  64.4 3.2 %collective-permute-done.19.refs_14_ = bf16[32,3072]{1,0:T(8,128)(2,1)S(1)} collective-permute-done((bf16[32,3072]{1,0:T(8,128)(2,1)S(1)}, bf16[32,3072]{1,0:T(8,128)(2,1)S(1)}, u32[]{:S(2)}, u32[]{:S(2)}) %collective-permute-start.19) | collective-permute-done | bytes 196640 | tf_op jit(solution)/shard_map/ppermute | solution.py:348
  70.8 15.4 %logits.1 = (f32[1024,1024]{1,0:T(8,128)S(1)}, f32[1024,1024]{1,0:T(8,128)S(1)}, f32[2,1024]{1,0:T(2,128)S(1)}, f32[2,1024]{1,0:T(2,128)S(1)}, bf16[1024,512]{1,...) custom-call(bf16[64,3072]{1,0:T(8,128)(2,1)S(1)} %copy-done.1, bf16[64,3072]{1,0:T(8,128)(2,1)S(1)} %collective-permute-done.refs_1_, ...), custom_call_target="tpu_custom_call" | custom-call | flops 9126805504 | bytes 20971520 | tf_op jit(solution)/shard_map/logits/pallas_call | solution.py:197
  86.8 2.0 %collective-permute-done.24 = f32[2,1024]{1,0:T(2,128)S(1)} collective-permute-done((f32[2,1024]{1,0:T(2,128)S(1)}, f32[2,1024]{1,0:T(2,128)S(1)}, u32[]{:S(2)}, u32[]{:S(2)}) %collective-permute-start.24) | collective-permute-done | bytes 8224 | tf_op jit(solution)/shard_map/ppermute | solution.py:353
  90.3 2.3 %collective-permute-done.25 = f32[2,1024]{1,0:T(2,128)S(1)} collective-permute-done((f32[2,1024]{1,0:T(2,128)S(1)}, f32[2,1024]{1,0:T(2,128)S(1)}, u32[]{:S(2)}, u32[]{:S(2)}) %collective-permute-start.25) | collective-permute-done | bytes 8224 | tf_op jit(solution)/shard_map/ppermute | solution.py:353
  97.2 2.3 %collective-permute-start.31 = (f32[2,1024]{1,0:T(2,128)S(1)}, f32[2,1024]{1,0:T(2,128)S(1)}, u32[]{:S(2)}, u32[]{:S(2)}) collective-permute-start(f32[2,1024]{1,0:T(2,128)S(1)} %multiply_add_fusion.1), channel_id=1, source_target_pairs={{0,134},{2,132},{4,130},{6,128},{128,6},{130,4},{132,2},{134,0},{1... | collective-permute-start | bytes 24584 | tf_op jit(solution)/shard_map/ppermute | solution.py:353
  101.0 6.5 %weights.1 = (bf16[1024,512]{1,0:T(8,128)(2,1)}, f32[512,512]{1,0:T(8,128)S(1)}, f32[512,512]{1,0:T(8,128)}) custom-call(f32[1024,1024]{1,0:T(8,128)S(1)} %get-tuple-element.70.t_ref, f32[1024,1024]{1,0:T(8,128)S(1)} %get-tuple-element.71.s_ref, f32[2,1024]{1,0:T(2,128)S(1)} %multiply_add_fusion.4.row_ref, f32[2,1024]{1,0:T(2,128)S(1)} %multiply_add_fusion.col_ref, ...), custom_call_target="tpu_custom_call" | custom-call | flops 2147483648 | bytes 10485760 | tf_op jit(solution)/shard_map/weights/pallas_call | solution.py:276
  107.5 5.3 %collective-permute-start.32 = (f32[512,512]{1,0:T(8,128)}, f32[512,512]{1,0:T(8,128)S(1)}, u32[]{:S(2)}, u32[]{:S(2)}) collective-permute-start(f32[512,512]{1,0:T(8,128)} %get-tuple-element.78), channel_id=1, source_target_pairs={{0,1},{1,0},{2,3},{3,2},{4,5},{5,4},{6,7},{7,6},{8,9},{9,8},{10,11... | collective-permute-start | bytes 3145736 | tf_op jit(solution)/shard_map/ppermute | solution.py:341
  112.8 3.9 %all-to-all-start = ((bf16[16,64,512]{2,1,0:T(8,128)(2,1)}), bf16[16,64,512]{2,1,0:T(8,128)(2,1)S(1)}, u32[]{:S(2)}, u32[]{:S(2)}) async-start(bf16[16,64,512]{2,1,0:T(8,128)(2,1)} %bitcast.5), calls=%async_computation | async-start | bytes 2097152 | tf_op jit(solution)/shard_map/all_to_all | solution.py:422
  116.8 2.0 %collective-permute-start.33 = (bf16[128,512]{1,0:T(8,128)(2,1)S(1)}, bf16[128,512]{1,0:T(8,128)(2,1)S(1)}, u32[]{:S(2)}, u32[]{:S(2)}) collective-permute-start(bf16[128,512]{1,0:T(8,128)(2,1)S(1)} %get-tuple-element.80), channel_id=1, source_target_pairs={{0,2},{1,135},{2,4},{3,1},{4,6},{5,3},{6,128},{7,5},{128,130},{129... | collective-permute-start | bytes 393224 | tf_op jit(solution)/shard_map/ppermute | solution.py:348
  118.8 2.7 %collective-permute-start.34 = (bf16[128,512]{1,0:T(8,128)(2,1)S(1)}, bf16[128,512]{1,0:T(8,128)(2,1)S(1)}, u32[]{:S(2)}, u32[]{:S(2)}) collective-permute-start(bf16[128,512]{1,0:T(8,128)(2,1)S(1)} %get-tuple-element.81), channel_id=1, source_target_pairs={{0,4},{1,133},{2,6},{3,135},{4,128},{5,1},{6,130},{7,3},{128,132},... | collective-permute-start | bytes 393224 | tf_op jit(solution)/shard_map/ppermute | solution.py:348
  121.6 1.8 %collective-permute-start.35 = (bf16[128,512]{1,0:T(8,128)(2,1)S(1)}, bf16[128,512]{1,0:T(8,128)(2,1)S(1)}, u32[]{:S(2)}, u32[]{:S(2)}) collective-permute-start(bf16[128,512]{1,0:T(8,128)(2,1)S(1)} %get-tuple-element.82), channel_id=1, source_target_pairs={{0,6},{1,131},{2,128},{3,133},{4,130},{5,135},{6,132},{7,1},{128,1... | collective-permute-start | bytes 393224 | tf_op jit(solution)/shard_map/ppermute | solution.py:348
  123.3 3.5 %collective-permute-start.36 = (bf16[64,512]{1,0:T(8,128)(2,1)S(1)}, bf16[64,512]{1,0:T(8,128)(2,1)S(1)}, u32[]{:S(2)}, u32[]{:S(2)}) collective-permute-start(bf16[64,512]{1,0:T(8,128)(2,1)S(1)} %get-tuple-element.83), channel_id=1, source_target_pairs={{0,128},{1,129},{2,130},{3,131},{4,132},{5,133},{6,134},{7,135},{1... | collective-permute-start | bytes 196616 | tf_op jit(solution)/shard_map/ppermute | solution.py:348
  126.9 4.6 %collective-permute-done.36 = bf16[64,512]{1,0:T(8,128)(2,1)S(1)} collective-permute-done((bf16[64,512]{1,0:T(8,128)(2,1)S(1)}, bf16[64,512]{1,0:T(8,128)(2,1)S(1)}, u32[]{:S(2)}, u32[]{:S(2)}) %collective-permute-start.36) | collective-permute-done | bytes 65568 | tf_op jit(solution)/shard_map/ppermute | solution.py:348
  131.6 4.1 %collective-permute-start.37 = (f32[64,512]{1,0:T(8,128)S(1)}, f32[64,512]{1,0:T(8,128)S(1)}, u32[]{:S(2)}, u32[]{:S(2)}) collective-permute-start(f32[64,512]{1,0:T(8,128)S(1)} %slice_add_fusion), channel_id=1, source_target_pairs={{0,1},{1,0},{2,3},{3,2},{4,5},{5,4},{6,7},{7,6},{8,9},{9,8},{10,11... | collective-permute-start | bytes 393224 | tf_op jit(solution)/shard_map/ppermute | solution.py:341
  (95 shorter events, 31.1 us)
Async XLA Ops:
  7.2 18.8 %collective-permute-start.6 = (bf16[2,64,3072]{2,1,0:T(8,128)(2,1)S(1)}, bf16[2,64,3072]{2,1,0:T(8,128)(2,1)S(1)}, u32[]{:S(2)}, u32[]{:S(2)}) collective-permute-start(bf16[2,64,3072]{2,1,0:T(8,128)(2,1)S(1)} %pair.1.refs_15_), channel_id=1, source_target_pairs={{0,2},{1,135},{2,4},{3,1},{4,6},{5,3},{6,128},{7,5},{128,130},{129... | collective-permute-start | bytes 2359304 | tf_op jit(solution)/shard_map/ppermute | solution.py:348
  11.2 12.2 %collective-permute-start.3 = (bf16[64,3072]{1,0:T(8,128)(2,1)S(1)}, bf16[64,3072]{1,0:T(8,128)(2,1)S(1)}, u32[]{:S(2)}, u32[]{:S(2)}) collective-permute-start(bf16[64,3072]{1,0:T(8,128)(2,1)S(1)} %copy-done.1), channel_id=1, source_target_pairs={{0,24},{1,9},{8,0},{9,17},{16,8},{17,25},{24,16},{25,1},{2,26},{3,... | collective-permute-start | bytes 1179656 | tf_op jit(solution)/shard_map/ppermute | solution.py:348
  12.5 10.9 %collective-permute-start.2 = (bf16[64,3072]{1,0:T(8,128)(2,1)S(1)}, bf16[64,3072]{1,0:T(8,128)(2,1)S(1)}, u32[]{:S(2)}, u32[]{:S(2)}) collective-permute-start(bf16[64,3072]{1,0:T(8,128)(2,1)S(1)} %copy-done.1), channel_id=1, source_target_pairs={{0,8},{1,25},{8,16},{9,1},{16,24},{17,9},{24,0},{25,17},{2,10},{3,... | collective-permute-start | bytes 1179656 | tf_op jit(solution)/shard_map/ppermute | solution.py:348
  13.9 12.1 %collective-permute-start.1 = (bf16[64,3072]{1,0:T(8,128)(2,1)S(1)}, bf16[64,3072]{1,0:T(8,128)(2,1)S(1)}, u32[]{:S(2)}, u32[]{:S(2)}) collective-permute-start(bf16[64,3072]{1,0:T(8,128)(2,1)S(1)} %copy-done.1), channel_id=1, source_target_pairs={{0,96},{1,33},{32,0},{33,65},{64,32},{65,97},{96,64},{97,1},{2,98}... | collective-permute-start | bytes 1179656 | tf_op jit(solution)/shard_map/ppermute | solution.py:348
  15.1 10.9 %collective-permute-start = (bf16[64,3072]{1,0:T(8,128)(2,1)S(1)}, bf16[64,3072]{1,0:T(8,128)(2,1)S(1)}, u32[]{:S(2)}, u32[]{:S(2)}) collective-permute-start(bf16[64,3072]{1,0:T(8,128)(2,1)S(1)} %copy-done.1), channel_id=1, source_target_pairs={{0,32},{1,97},{32,64},{33,1},{64,96},{65,33},{96,0},{97,65},{2,34}... | collective-permute-start | bytes 1179656 | tf_op jit(solution)/shard_map/ppermute | solution.py:348
  26.8 17.2 %collective-permute-start.9 = (bf16[128,3072]{1,0:T(8,128)(2,1)S(1)}, bf16[128,3072]{1,0:T(8,128)(2,1)S(1)}, u32[]{:S(2)}, u32[]{:S(2)}) collective-permute-start(bf16[128,3072]{1,0:T(8,128)(2,1)S(1)} %pad_maximum_fusion.1), channel_id=1, source_target_pairs={{0,8},{1,25},{8,16},{9,1},{16,24},{17,9},{24,0},{25,17},{2,10},{3,... | collective-permute-start | bytes 2359304 | tf_op jit(solution)/shard_map/ppermute | solution.py:348
  28.4 15.7 %collective-permute-start.7 = (bf16[128,3072]{1,0:T(8,128)(2,1)S(1)}, bf16[128,3072]{1,0:T(8,128)(2,1)S(1)}, u32[]{:S(2)}, u32[]{:S(2)}) collective-permute-start(bf16[128,3072]{1,0:T(8,128)(2,1)S(1)} %pad_maximum_fusion), channel_id=1, source_target_pairs={{0,32},{1,97},{32,64},{33,1},{64,96},{65,33},{96,0},{97,65},{2,34}... | collective-permute-start | bytes 2359304 | tf_op jit(solution)/shard_map/ppermute | solution.py:348
  29.4 14.7 %collective-permute-start.12 = (bf16[2,64,3072]{2,1,0:T(8,128)(2,1)S(1)}, bf16[2,64,3072]{2,1,0:T(8,128)(2,1)S(1)}, u32[]{:S(2)}, u32[]{:S(2)}) collective-permute-start(bf16[2,64,3072]{2,1,0:T(8,128)(2,1)S(1)} %collective-permute-done.6.refs_16_), channel_id=1, source_target_pairs={{0,2},{1,135},{2,4},{3,1},{4,6},{5,3},{6,128},{7,5},{128,130},{129... | collective-permute-start | bytes 2359304 | tf_op jit(solution)/shard_map/ppermute | solution.py:348
  32.0 11.8 %collective-permute-start.10 = (bf16[64,3072]{1,0:T(8,128)(2,1)S(1)}, bf16[64,3072]{1,0:T(8,128)(2,1)S(1)}, u32[]{:S(2)}, u32[]{:S(2)}) collective-permute-start(bf16[64,3072]{1,0:T(8,128)(2,1)S(1)} %pad_maximum_fusion.5), channel_id=1, source_target_pairs={{0,24},{1,9},{8,0},{9,17},{16,8},{17,25},{24,16},{25,1},{2,26},{3,... | collective-permute-start | bytes 1179656 | tf_op jit(solution)/shard_map/ppermute | solution.py:348
  32.1 11.9 %collective-permute-start.8 = (bf16[64,3072]{1,0:T(8,128)(2,1)S(1)}, bf16[64,3072]{1,0:T(8,128)(2,1)S(1)}, u32[]{:S(2)}, u32[]{:S(2)}) collective-permute-start(bf16[64,3072]{1,0:T(8,128)(2,1)S(1)} %pad_maximum_fusion.4), channel_id=1, source_target_pairs={{0,96},{1,33},{32,0},{33,65},{64,32},{65,97},{96,64},{97,1},{2,98}... | collective-permute-start | bytes 1179656 | tf_op jit(solution)/shard_map/ppermute | solution.py:348
  44.2 13.3 %collective-permute-start.15 = (bf16[96,3072]{1,0:T(8,128)(2,1)S(1)}, bf16[96,3072]{1,0:T(8,128)(2,1)S(1)}, u32[]{:S(2)}, u32[]{:S(2)}) collective-permute-start(bf16[96,3072]{1,0:T(8,128)(2,1)S(1)} %pad_maximum_fusion.3), channel_id=1, source_target_pairs={{0,8},{1,25},{8,16},{9,1},{16,24},{17,9},{24,0},{25,17},{2,10},{3,... | collective-permute-start | bytes 1769480 | tf_op jit(solution)/shard_map/ppermute | solution.py:348
  47.0 11.5 %collective-permute-start.17 = (bf16[2,64,3072]{2,1,0:T(8,128)(2,1)S(1)}, bf16[2,64,3072]{2,1,0:T(8,128)(2,1)S(1)}, u32[]{:S(2)}, u32[]{:S(2)}) collective-permute-start(bf16[2,64,3072]{2,1,0:T(8,128)(2,1)S(1)} %collective-permute-done.12.refs_17_), channel_id=1, source_target_pairs={{0,2},{1,135},{2,4},{3,1},{4,6},{5,3},{6,128},{7,5},{128,130},{129... | collective-permute-start | bytes 2359304 | tf_op jit(solution)/shard_map/ppermute | solution.py:348
  48.1 10.4 %collective-permute-start.13 = (bf16[96,3072]{1,0:T(8,128)(2,1)S(1)}, bf16[96,3072]{1,0:T(8,128)(2,1)S(1)}, u32[]{:S(2)}, u32[]{:S(2)}) collective-permute-start(bf16[96,3072]{1,0:T(8,128)(2,1)S(1)} %pad_maximum_fusion.2), channel_id=1, source_target_pairs={{0,32},{1,97},{32,64},{33,1},{64,96},{65,33},{96,0},{97,65},{2,34}... | collective-permute-start | bytes 1769480 | tf_op jit(solution)/shard_map/ppermute | solution.py:348
  49.1 8.2 %collective-permute-start.14 = (bf16[32,3072]{1,0:T(8,128)(2,1)S(1)}, bf16[32,3072]{1,0:T(8,128)(2,1)S(1)}, u32[]{:S(2)}, u32[]{:S(2)}) collective-permute-start(bf16[32,3072]{1,0:T(8,128)(2,1)S(1)} %slice.64), channel_id=1, source_target_pairs={{0,96},{1,33},{32,0},{33,65},{64,32},{65,97},{96,64},{97,1},{2,98}... | collective-permute-start | bytes 589832 | tf_op jit(solution)/shard_map/ppermute | solution.py:348
  49.8 7.7 %collective-permute-start.16 = (bf16[32,3072]{1,0:T(8,128)(2,1)S(1)}, bf16[32,3072]{1,0:T(8,128)(2,1)S(1)}, u32[]{:S(2)}, u32[]{:S(2)}) collective-permute-start(bf16[32,3072]{1,0:T(8,128)(2,1)S(1)} %slice.66), channel_id=1, source_target_pairs={{0,24},{1,9},{8,0},{9,17},{16,8},{17,25},{24,16},{25,1},{2,26},{3,... | collective-permute-start | bytes 589832 | tf_op jit(solution)/shard_map/ppermute | solution.py:348
  57.3 7.0 %collective-permute-start.21 = (bf16[2,64,3072]{2,1,0:T(8,128)(2,1)S(1)}, bf16[2,64,3072]{2,1,0:T(8,128)(2,1)S(1)}, u32[]{:S(2)}, u32[]{:S(2)}) collective-permute-start(bf16[2,64,3072]{2,1,0:T(8,128)(2,1)S(1)} %collective-permute-done.12.refs_17_), channel_id=1, source_target_pairs={{0,1},{1,0},{2,3},{3,2},{4,5},{5,4},{6,7},{7,6},{8,9},{9,8},{10,11... | collective-permute-start | bytes 2359304 | tf_op jit(solution)/shard_map/ppermute | solution.py:341
  58.5 9.6 %collective-permute-start.22 = (bf16[2,64,3072]{2,1,0:T(8,128)(2,1)S(1)}, bf16[2,64,3072]{2,1,0:T(8,128)(2,1)S(1)}, u32[]{:S(2)}, u32[]{:S(2)}) collective-permute-start(bf16[2,64,3072]{2,1,0:T(8,128)(2,1)S(1)} %collective-permute-done.17.refs_18_), channel_id=1, source_target_pairs={{0,1},{1,0},{2,3},{3,2},{4,5},{5,4},{6,7},{7,6},{8,9},{9,8},{10,11... | collective-permute-start | bytes 2359304 | tf_op jit(solution)/shard_map/ppermute | solution.py:341
  60.1 8.0 %collective-permute-start.20 = (bf16[64,3072]{1,0:T(8,128)(2,1)S(1)}, bf16[64,3072]{1,0:T(8,128)(2,1)S(1)}, u32[]{:S(2)}, u32[]{:S(2)}) collective-permute-start(bf16[64,3072]{1,0:T(8,128)(2,1)S(1)} %slice_bitcast_fusion), channel_id=1, source_target_pairs={{0,2},{1,135},{2,4},{3,1},{4,6},{5,3},{6,128},{7,5},{128,130},{129... | collective-permute-start | bytes 1179656 | tf_op jit(solution)/shard_map/ppermute | solution.py:348
  107.5 9.2 %collective-permute-start.32 = (f32[512,512]{1,0:T(8,128)}, f32[512,512]{1,0:T(8,128)S(1)}, u32[]{:S(2)}, u32[]{:S(2)}) collective-permute-start(f32[512,512]{1,0:T(8,128)} %get-tuple-element.78), channel_id=1, source_target_pairs={{0,1},{1,0},{2,3},{3,2},{4,5},{5,4},{6,7},{7,6},{8,9},{9,8},{10,11... | collective-permute-start | bytes 3145736 | tf_op jit(solution)/shard_map/ppermute | solution.py:341
  112.8 23.0 %all-to-all-start = ((bf16[16,64,512]{2,1,0:T(8,128)(2,1)}), bf16[16,64,512]{2,1,0:T(8,128)(2,1)S(1)}, u32[]{:S(2)}, u32[]{:S(2)}) async-start(bf16[16,64,512]{2,1,0:T(8,128)(2,1)} %bitcast.5), calls=%async_computation | async-start | bytes 2097152 | tf_op jit(solution)/shard_map/all_to_all | solution.py:422
  116.8 14.7 %collective-permute-start.33 = (bf16[128,512]{1,0:T(8,128)(2,1)S(1)}, bf16[128,512]{1,0:T(8,128)(2,1)S(1)}, u32[]{:S(2)}, u32[]{:S(2)}) collective-permute-start(bf16[128,512]{1,0:T(8,128)(2,1)S(1)} %get-tuple-element.80), channel_id=1, source_target_pairs={{0,2},{1,135},{2,4},{3,1},{4,6},{5,3},{6,128},{7,5},{128,130},{129... | collective-permute-start | bytes 393224 | tf_op jit(solution)/shard_map/ppermute | solution.py:348
  118.8 12.7 %collective-permute-start.34 = (bf16[128,512]{1,0:T(8,128)(2,1)S(1)}, bf16[128,512]{1,0:T(8,128)(2,1)S(1)}, u32[]{:S(2)}, u32[]{:S(2)}) collective-permute-start(bf16[128,512]{1,0:T(8,128)(2,1)S(1)} %get-tuple-element.81), channel_id=1, source_target_pairs={{0,4},{1,133},{2,6},{3,135},{4,128},{5,1},{6,130},{7,3},{128,132},... | collective-permute-start | bytes 393224 | tf_op jit(solution)/shard_map/ppermute | solution.py:348
  121.6 9.9 %collective-permute-start.35 = (bf16[128,512]{1,0:T(8,128)(2,1)S(1)}, bf16[128,512]{1,0:T(8,128)(2,1)S(1)}, u32[]{:S(2)}, u32[]{:S(2)}) collective-permute-start(bf16[128,512]{1,0:T(8,128)(2,1)S(1)} %get-tuple-element.82), channel_id=1, source_target_pairs={{0,6},{1,131},{2,128},{3,133},{4,130},{5,135},{6,132},{7,1},{128,1... | collective-permute-start | bytes 393224 | tf_op jit(solution)/shard_map/ppermute | solution.py:348
  123.3 8.2 %collective-permute-start.36 = (bf16[64,512]{1,0:T(8,128)(2,1)S(1)}, bf16[64,512]{1,0:T(8,128)(2,1)S(1)}, u32[]{:S(2)}, u32[]{:S(2)}) collective-permute-start(bf16[64,512]{1,0:T(8,128)(2,1)S(1)} %get-tuple-element.83), channel_id=1, source_target_pairs={{0,128},{1,129},{2,130},{3,131},{4,132},{5,133},{6,134},{7,135},{1... | collective-permute-start | bytes 196616 | tf_op jit(solution)/shard_map/ppermute | solution.py:348
  (17 other events, 61.4 us)

commit v2 on v1

--- a/solution.py
+++ b/solution.py
@@ -179,7 +179,7 @@
                 col_ref[k : k + 1, here] = log2_sum(value, 0)
             return 0
 
-        lax.fori_loop(0, n // tile, columns, 0)
+        lax.fori_loop(0, n // tile, columns, 0, unroll=2)
         lanes = lax.broadcasted_iota(jnp.int32, (128, 128), 1)
 
         def row_sums(i, _):
@@ -223,79 +223,70 @@
 def weights(t, s, row_lse, col_lse, srow, scol, share, ring):
     m, n = t.shape
     ds = srow.shape[1]
-    block = 512
+    block = 256
 
     def kernel(
-        t_ref, s_ref, row_ref, col_ref, srow_ref, scol_ref, img_ref, mine_ref, theirs_ref, lse, acc
+        t_ref, s_ref, row_ref, col_ref, srow_ref, scol_ref, img_ref, mine_ref, theirs_ref, *bufs
     ):
-        step = pl.program_id(0)
-
-        @pl.when(step == 0)
-        def _():
-            lse[...] = jnp.transpose(
-                jnp.concatenate([row_ref[...], jnp.zeros((126, m), F32)], axis=0)
-            )
-
-        t = t_ref[...]
-        s = s_ref[...]
-        row = lse[pl.ds(pl.multiple_of(step * block, block), block), :]
-        along_rows = jnp.exp2(s - row[:, 1:2]) - jnp.exp2(t - row[:, 0:1])
-        along_cols = jnp.exp2(s - col_ref[1:2, :]) - jnp.exp2(t - col_ref[0:1, :])
-        w = (weight_scale * (along_rows + along_cols)).astype(BF16)
-        part = tn(w, srow_ref[...])
-        img_ref[...] = jnp.dot(w, scol_ref[...], preferred_element_type=F32).astype(BF16)
-
-        @pl.when(step == 0)
-        def _():
-            acc[...] = part
-
-        @pl.when(step > 0)
-        def _():
-            acc[...] += part
-
-        @pl.when(step == pl.num_programs(0) - 1)
-        def _():
-            z = lax.axis_index(RING)
-            sign = 1 - 2 * lax.axis_index("core")
-
-            def terms(ahead, other):
-                at = lax.rem(z + ahead + ring, ring) * share + other * ring * share
-                return acc[pl.ds(pl.multiple_of(at, share), share), :]
-
-            half = ring // 2
-            slots = [(k, h) for k in range(1, half) for h in (0, 1)]
-            for i, (k, h) in enumerate(slots):
-                here = slice(i * share, (i + 1) * share)
-                mine_ref[here, :] = terms(sign * k, h)
-                theirs_ref[here, :] = terms(-sign * k, 1 - h)
-            for i, k in enumerate((half, 0)):
-                here = slice((ring - 2 + i) * share, (ring - 1 + i) * share)
-                mine_ref[here, :] = terms(k, 0)
-                theirs_ref[here, :] = terms(k, 1)
-
-    return pl.pallas_call(
-        kernel,
-        grid=(m // block,),
-        in_specs=[
-            pl.BlockSpec((block, n), lambda i: (i, 0)),
-            pl.BlockSpec((block, n), lambda i: (i, 0)),
-            pl.BlockSpec((2, m), lambda i: (0, 0)),
-            pl.BlockSpec((2, n), lambda i: (0, 0)),
-            pl.BlockSpec((block, ds), lambda i: (i, 0)),
-            pl.BlockSpec((n, ds), lambda i: (0, 0)),
-        ],
-        out_specs=[
-            pl.BlockSpec((block, ds), lambda i: (i, 0)),
-            pl.BlockSpec((n // 2, ds), lambda i: (0, 0)),
-            pl.BlockSpec((n // 2, ds), lambda i: (0, 0)),
-        ],
+        lse, w_buf, acc = bufs
+        lse[...] = jnp.transpose(jnp.concatenate([row_ref[...], jnp.zeros((126, m), F32)], axis=0))
+
+        def some_rows(i, _):
+            here = pl.ds(pl.multiple_of(i * block, block), block)
+            t = t_ref[here, :]
+            s = s_ref[here, :]
+            row = lse[here, :]
+            along_rows = jnp.exp2(s - row[:, 1:2]) - jnp.exp2(t - row[:, 0:1])
+            along_cols = jnp.exp2(s - col_ref[1:2, :]) - jnp.exp2(t - col_ref[0:1, :])
+            w = (weight_scale * (along_rows + along_cols)).astype(BF16)
+            w_buf[here, :] = w
+            img_ref[here, :] = jnp.dot(
+                w, scol_ref[...], preferred_element_type=F32
+            ).astype(BF16)
+            return 0
+
+        lax.fori_loop(0, m // block, some_rows, 0, unroll=2)
+
+        def some_cols(i, _):
+            here = pl.ds(pl.multiple_of(i * block, block), block)
+            acc[here, :] = tn(w_buf[:, here], srow_ref[...])
+            return 0
+
+        lax.fori_loop(0, n // block, some_cols, 0)
+
+        z = lax.axis_index(RING)
+        sign = 1 - 2 * lax.axis_index("core")
+
+        def terms(ahead, other):
+            at = lax.rem(z + ahead + ring, ring) * share + other * ring * share
+            return acc[pl.ds(pl.multiple_of(at, share), share), :]
+
+        half = ring // 2
+        slots = [(k, h) for k in range(1, half) for h in (0, 1)]
+        for i, (k, h) in enumerate(slots):
+            here = slice(i * share, (i + 1) * share)
+            mine_ref[here, :] = terms(sign * k, h)
+            theirs_ref[here, :] = terms(-sign * k, 1 - h)
+        for i, k in enumerate((half, 0)):
+            here = slice((ring - 2 + i) * share, (ring - 1 + i) * share)
+            mine_ref[here, :] = terms(k, 0)
+            theirs_ref[here, :] = terms(k, 1)
+
+    return pl.pallas_call(
+        kernel,
+        in_specs=[VMEM] * 6,
+        out_specs=[VMEM] * 3,
         out_shape=[
             jax.ShapeDtypeStruct((m, ds), BF16),
             jax.ShapeDtypeStruct((n // 2, ds), F32),
             jax.ShapeDtypeStruct((n // 2, ds), F32),
         ],
-        scratch_shapes=[pltpu.VMEM((m, 128), F32), pltpu.VMEM((n, ds), F32)],
-        compiler_params=pltpu.CompilerParams(vmem_limit_bytes=20 * MIB),
+        scratch_shapes=[
+            pltpu.VMEM((m, 128), F32),
+            pltpu.VMEM((m, n), BF16),
+            pltpu.VMEM((n, ds), F32),
+        ],
+        compiler_params=pltpu.CompilerParams(vmem_limit_bytes=28 * MIB),
         cost_estimate=pl.CostEstimate(
             flops=4 * m * n * ds, bytes_accessed=10 * m * n, transcendentals=4 * m * n
         ),

time: 138 us -> 137 us (level)
  no operation moved by 1% of the time
where the time goes in v2:
time: 137 us
  starting transfers between devices  61.8 us (45%)
  waiting for transfers between devices  47.1 us (34%)
  Pallas kernels  24.2 us (18%)
    ppermute x22, waiting for transfers between devices, turn(): return lax.ppermute(x, axes, pairs)  38.1 us
    ppermute x22, starting transfers between devices, turn(): return lax.ppermute(x, axes, pairs)  34.7 us
    ppermute x9, starting transfers between devices, swap(): return lax.ppermute(x, 'core', [(0, 1), (1, 0)])  16.6 us
    pallas_call x1, Pallas kernels, logits(): pl.pallas_call(kernel, in_specs=[VMEM] * (n_rows + n_cols), out_specs=[VM...  14.8 us
    ppermute x7, waiting for transfers between devices, join_along(): return join(x, lax.ppermute(x, axis, [(i, i ^ step) for i in range(n)]))  7.51 us
    ppermute x7, starting transfers between devices, join_along(): return join(x, lax.ppermute(x, axis, [(i, i ^ step) for i in range(n)]))  6.52 us
    pallas_call x1, Pallas kernels, weights(): pl.pallas_call(kernel, in_specs=[VMEM] * 6, out_specs=[VMEM] * 3, out_sha...  6.28 us
    all_to_all x1, starting transfers between devices, local(): img_sent = lax.all_to_all(img.reshape(-1, share, ds), PLANE, 0, 0)  3.94 us
  transfers between devices with their start and end apart: 39, of which 17 were waited for; matrix products, arithmetic and copies ran while one was open for 0% of the time, Pallas kernels for 2%

profile of v2, /device:TPU:1, one launch (start us, length us, event | category | flops | bytes accessed | tf_op | source)
XLA Modules:
  0.0 136.5 jit_solution(15196453100585687571)
XLA Ops:
  0.6 3.3 %collective-permute-start.4 = (f32[64,1280]{1,0:T(8,128)}, f32[64,1280]{1,0:T(8,128)S(1)}, u32[]{:S(2)}, u32[]{:S(2)}) collective-permute-start(f32[64,1280]{1,0:T(8,128)} %bitcast.11), channel_id=1, source_target_pairs={{0,1},{1,0},{2,3},{3,2},{4,5},{5,4},{6,7},{7,6},{8,9},{9,8},{10,11... | collective-permute-start | bytes 983048 | tf_op jit(solution)/shard_map/ppermute | solution.py:332
  4.1 2.1 %pack.1 = (bf16[64,3072]{1,0:T(8,128)(2,1)}, bf16[64,3072]{1,0:T(8,128)(2,1)}) custom-call(f32[64,1280]{1,0:T(8,128)} %bitcast.10, bf16[64,512]{1,0:T(8,128)(2,1)} %bitcast.14, f32[64,1280]{1,0:T(8,128)} %bitcast.12, bf16[64,512]{1,0:T(8,128)(2,1)} %bitcast.16), custom_call_target="tpu_custom_call" | custom-call | tf_op jit(solution)/shard_map/pack/pallas_call | solution.py:66
  7.2 3.9 %collective-permute-start.6 = (bf16[2,64,3072]{2,1,0:T(8,128)(2,1)S(1)}, bf16[2,64,3072]{2,1,0:T(8,128)(2,1)S(1)}, u32[]{:S(2)}, u32[]{:S(2)}) collective-permute-start(bf16[2,64,3072]{2,1,0:T(8,128)(2,1)S(1)} %pair.1.refs_15_), channel_id=1, source_target_pairs={{0,2},{1,135},{2,4},{3,1},{4,6},{5,3},{6,128},{7,5},{128,130},{129... | collective-permute-start | bytes 2359304 | tf_op jit(solution)/shard_map/ppermute | solution.py:339
  16.6 6.8 %collective-permute-done.3.refs_4_ = bf16[64,3072]{1,0:T(8,128)(2,1)S(1)} collective-permute-done((bf16[64,3072]{1,0:T(8,128)(2,1)S(1)}, bf16[64,3072]{1,0:T(8,128)(2,1)S(1)}, u32[]{:S(2)}, u32[]{:S(2)}) %collective-permute-start.3) | collective-permute-done | bytes 393248 | tf_op jit(solution)/shard_map/ppermute | solution.py:339
  23.4 2.6 %collective-permute-done.1.refs_2_ = bf16[64,3072]{1,0:T(8,128)(2,1)S(1)} collective-permute-done((bf16[64,3072]{1,0:T(8,128)(2,1)S(1)}, bf16[64,3072]{1,0:T(8,128)(2,1)S(1)}, u32[]{:S(2)}, u32[]{:S(2)}) %collective-permute-start.1) | collective-permute-done | bytes 393248 | tf_op jit(solution)/shard_map/ppermute | solution.py:339
  29.4 2.6 %collective-permute-start.12 = (bf16[2,64,3072]{2,1,0:T(8,128)(2,1)S(1)}, bf16[2,64,3072]{2,1,0:T(8,128)(2,1)S(1)}, u32[]{:S(2)}, u32[]{:S(2)}) collective-permute-start(bf16[2,64,3072]{2,1,0:T(8,128)(2,1)S(1)} %collective-permute-done.6.refs_16_), channel_id=1, source_target_pairs={{0,2},{1,135},{2,4},{3,1},{4,6},{5,3},{6,128},{7,5},{128,130},{129... | collective-permute-start | bytes 2359304 | tf_op jit(solution)/shard_map/ppermute | solution.py:339
  32.2 11.7 %collective-permute-done.10.refs_8_ = bf16[64,3072]{1,0:T(8,128)(2,1)S(1)} collective-permute-done((bf16[64,3072]{1,0:T(8,128)(2,1)S(1)}, bf16[64,3072]{1,0:T(8,128)(2,1)S(1)}, u32[]{:S(2)}, u32[]{:S(2)}) %collective-permute-start.10) | collective-permute-done | bytes 393248 | tf_op jit(solution)/shard_map/ppermute | solution.py:339
  44.2 2.8 %collective-permute-start.15 = (bf16[96,3072]{1,0:T(8,128)(2,1)S(1)}, bf16[96,3072]{1,0:T(8,128)(2,1)S(1)}, u32[]{:S(2)}, u32[]{:S(2)}) collective-permute-start(bf16[96,3072]{1,0:T(8,128)(2,1)S(1)} %pad_maximum_fusion.3), channel_id=1, source_target_pairs={{0,8},{1,25},{8,16},{9,1},{16,24},{17,9},{24,0},{25,17},{2,10},{3,... | collective-permute-start | bytes 1769480 | tf_op jit(solution)/shard_map/ppermute | solution.py:339
  49.9 7.4 %collective-permute-done.14.refs_10_ = bf16[32,3072]{1,0:T(8,128)(2,1)S(1)} collective-permute-done((bf16[32,3072]{1,0:T(8,128)(2,1)S(1)}, bf16[32,3072]{1,0:T(8,128)(2,1)S(1)}, u32[]{:S(2)}, u32[]{:S(2)}) %collective-permute-start.14) | collective-permute-done | bytes 196640 | tf_op jit(solution)/shard_map/ppermute | solution.py:339
  60.1 2.5 %collective-permute-start.20 = (bf16[64,3072]{1,0:T(8,128)(2,1)S(1)}, bf16[64,3072]{1,0:T(8,128)(2,1)S(1)}, u32[]{:S(2)}, u32[]{:S(2)}) collective-permute-start(bf16[64,3072]{1,0:T(8,128)(2,1)S(1)} %slice_bitcast_fusion), channel_id=1, source_target_pairs={{0,2},{1,135},{2,4},{3,1},{4,6},{5,3},{6,128},{7,5},{128,130},{129... | collective-permute-start | bytes 1179656 | tf_op jit(solution)/shard_map/ppermute | solution.py:339
  64.4 3.2 %collective-permute-done.19.refs_14_ = bf16[32,3072]{1,0:T(8,128)(2,1)S(1)} collective-permute-done((bf16[32,3072]{1,0:T(8,128)(2,1)S(1)}, bf16[32,3072]{1,0:T(8,128)(2,1)S(1)}, u32[]{:S(2)}, u32[]{:S(2)}) %collective-permute-start.19) | collective-permute-done | bytes 196640 | tf_op jit(solution)/shard_map/ppermute | solution.py:339
  70.8 14.8 %logits.1 = (f32[1024,1024]{1,0:T(8,128)S(1)}, f32[1024,1024]{1,0:T(8,128)S(1)}, f32[2,1024]{1,0:T(2,128)S(1)}, f32[2,1024]{1,0:T(2,128)S(1)}, bf16[1024,512]{1,...) custom-call(bf16[64,3072]{1,0:T(8,128)(2,1)S(1)} %copy-done.1, bf16[64,3072]{1,0:T(8,128)(2,1)S(1)} %collective-permute-done.refs_1_, ...), custom_call_target="tpu_custom_call" | custom-call | flops 9126805504 | bytes 20971520 | tf_op jit(solution)/shard_map/logits/pallas_call | solution.py:197
  86.2 2.0 %collective-permute-done.24 = f32[2,1024]{1,0:T(2,128)S(1)} collective-permute-done((f32[2,1024]{1,0:T(2,128)S(1)}, f32[2,1024]{1,0:T(2,128)S(1)}, u32[]{:S(2)}, u32[]{:S(2)}) %collective-permute-start.24) | collective-permute-done | bytes 8224 | tf_op jit(solution)/shard_map/ppermute | solution.py:344
  90.0 2.3 %collective-permute-done.25 = f32[2,1024]{1,0:T(2,128)S(1)} collective-permute-done((f32[2,1024]{1,0:T(2,128)S(1)}, f32[2,1024]{1,0:T(2,128)S(1)}, u32[]{:S(2)}, u32[]{:S(2)}) %collective-permute-start.25) | collective-permute-done | bytes 8224 | tf_op jit(solution)/shard_map/ppermute | solution.py:344
  96.6 2.3 %collective-permute-start.31 = (f32[2,1024]{1,0:T(2,128)S(1)}, f32[2,1024]{1,0:T(2,128)S(1)}, u32[]{:S(2)}, u32[]{:S(2)}) collective-permute-start(f32[2,1024]{1,0:T(2,128)S(1)} %multiply_add_fusion.1), channel_id=1, source_target_pairs={{0,134},{2,132},{4,130},{6,128},{128,6},{130,4},{132,2},{134,0},{1... | collective-permute-start | bytes 24584 | tf_op jit(solution)/shard_map/ppermute | solution.py:344
  100.5 6.3 %weights.1 = (bf16[1024,512]{1,0:T(8,128)(2,1)}, f32[512,512]{1,0:T(8,128)S(1)}, f32[512,512]{1,0:T(8,128)}) custom-call(f32[1024,1024]{1,0:T(8,128)S(1)} %get-tuple-element.70.t_ref, f32[1024,1024]{1,0:T(8,128)S(1)} %get-tuple-element.71.s_ref, f32[2,1024]{1,0:T(2,128)S(1)} %multiply_add_fusion.4.row_ref, f32[2,1024]{1,0:T(2,128)S(1)} %multiply_add_fusion.col_ref, ...), custom_call_target="tpu_custom_call" | custom-call | flops 2147483648 | bytes 10485760 | tf_op jit(solution)/shard_map/weights/pallas_call | solution.py:275
  106.8 5.3 %collective-permute-start.32 = (f32[512,512]{1,0:T(8,128)}, f32[512,512]{1,0:T(8,128)S(1)}, u32[]{:S(2)}, u32[]{:S(2)}) collective-permute-start(f32[512,512]{1,0:T(8,128)} %get-tuple-element.78), channel_id=1, source_target_pairs={{0,1},{1,0},{2,3},{3,2},{4,5},{5,4},{6,7},{7,6},{8,9},{9,8},{10,11... | collective-permute-start | bytes 3145736 | tf_op jit(solution)/shard_map/ppermute | solution.py:332
  112.0 3.9 %all-to-all-start = ((bf16[16,64,512]{2,1,0:T(8,128)(2,1)}), bf16[16,64,512]{2,1,0:T(8,128)(2,1)S(1)}, u32[]{:S(2)}, u32[]{:S(2)}) async-start(bf16[16,64,512]{2,1,0:T(8,128)(2,1)} %bitcast.5), calls=%async_computation | async-start | bytes 2097152 | tf_op jit(solution)/shard_map/all_to_all | solution.py:413
  116.1 2.1 %collective-permute-start.33 = (bf16[128,512]{1,0:T(8,128)(2,1)S(1)}, bf16[128,512]{1,0:T(8,128)(2,1)S(1)}, u32[]{:S(2)}, u32[]{:S(2)}) collective-permute-start(bf16[128,512]{1,0:T(8,128)(2,1)S(1)} %get-tuple-element.80), channel_id=1, source_target_pairs={{0,2},{1,135},{2,4},{3,1},{4,6},{5,3},{6,128},{7,5},{128,130},{129... | collective-permute-start | bytes 393224 | tf_op jit(solution)/shard_map/ppermute | solution.py:339
  118.2 2.7 %collective-permute-start.34 = (bf16[128,512]{1,0:T(8,128)(2,1)S(1)}, bf16[128,512]{1,0:T(8,128)(2,1)S(1)}, u32[]{:S(2)}, u32[]{:S(2)}) collective-permute-start(bf16[128,512]{1,0:T(8,128)(2,1)S(1)} %get-tuple-element.81), channel_id=1, source_target_pairs={{0,4},{1,133},{2,6},{3,135},{4,128},{5,1},{6,130},{7,3},{128,132},... | collective-permute-start | bytes 393224 | tf_op jit(solution)/shard_map/ppermute | solution.py:339
  120.8 1.7 %collective-permute-start.35 = (bf16[128,512]{1,0:T(8,128)(2,1)S(1)}, bf16[128,512]{1,0:T(8,128)(2,1)S(1)}, u32[]{:S(2)}, u32[]{:S(2)}) collective-permute-start(bf16[128,512]{1,0:T(8,128)(2,1)S(1)} %get-tuple-element.82), channel_id=1, source_target_pairs={{0,6},{1,131},{2,128},{3,133},{4,130},{5,135},{6,132},{7,1},{128,1... | collective-permute-start | bytes 393224 | tf_op jit(solution)/shard_map/ppermute | solution.py:339
  122.6 3.7 %collective-permute-start.36 = (bf16[64,512]{1,0:T(8,128)(2,1)S(1)}, bf16[64,512]{1,0:T(8,128)(2,1)S(1)}, u32[]{:S(2)}, u32[]{:S(2)}) collective-permute-start(bf16[64,512]{1,0:T(8,128)(2,1)S(1)} %get-tuple-element.83), channel_id=1, source_target_pairs={{0,128},{1,129},{2,130},{3,131},{4,132},{5,133},{6,134},{7,135},{1... | collective-permute-start | bytes 196616 | tf_op jit(solution)/shard_map/ppermute | solution.py:339
  126.3 4.5 %collective-permute-done.36 = bf16[64,512]{1,0:T(8,128)(2,1)S(1)} collective-permute-done((bf16[64,512]{1,0:T(8,128)(2,1)S(1)}, bf16[64,512]{1,0:T(8,128)(2,1)S(1)}, u32[]{:S(2)}, u32[]{:S(2)}) %collective-permute-start.36) | collective-permute-done | bytes 65568 | tf_op jit(solution)/shard_map/ppermute | solution.py:339
  130.9 3.9 %collective-permute-start.37 = (f32[64,512]{1,0:T(8,128)S(1)}, f32[64,512]{1,0:T(8,128)S(1)}, u32[]{:S(2)}, u32[]{:S(2)}) collective-permute-start(f32[64,512]{1,0:T(8,128)S(1)} %slice_add_fusion), channel_id=1, source_target_pairs={{0,1},{1,0},{2,3},{3,2},{4,5},{5,4},{6,7},{7,6},{8,9},{9,8},{10,11... | collective-permute-start | bytes 393224 | tf_op jit(solution)/shard_map/ppermute | solution.py:332
  (95 shorter events, 31.1 us)
Async XLA Ops:
  7.2 18.8 %collective-permute-start.6 = (bf16[2,64,3072]{2,1,0:T(8,128)(2,1)S(1)}, bf16[2,64,3072]{2,1,0:T(8,128)(2,1)S(1)}, u32[]{:S(2)}, u32[]{:S(2)}) collective-permute-start(bf16[2,64,3072]{2,1,0:T(8,128)(2,1)S(1)} %pair.1.refs_15_), channel_id=1, source_target_pairs={{0,2},{1,135},{2,4},{3,1},{4,6},{5,3},{6,128},{7,5},{128,130},{129... | collective-permute-start | bytes 2359304 | tf_op jit(solution)/shard_map/ppermute | solution.py:339
  11.2 12.2 %collective-permute-start.3 = (bf16[64,3072]{1,0:T(8,128)(2,1)S(1)}, bf16[64,3072]{1,0:T(8,128)(2,1)S(1)}, u32[]{:S(2)}, u32[]{:S(2)}) collective-permute-start(bf16[64,3072]{1,0:T(8,128)(2,1)S(1)} %copy-done.1), channel_id=1, source_target_pairs={{0,24},{1,9},{8,0},{9,17},{16,8},{17,25},{24,16},{25,1},{2,26},{3,... | collective-permute-start | bytes 1179656 | tf_op jit(solution)/shard_map/ppermute | solution.py:339
  12.5 10.9 %collective-permute-start.2 = (bf16[64,3072]{1,0:T(8,128)(2,1)S(1)}, bf16[64,3072]{1,0:T(8,128)(2,1)S(1)}, u32[]{:S(2)}, u32[]{:S(2)}) collective-permute-start(bf16[64,3072]{1,0:T(8,128)(2,1)S(1)} %copy-done.1), channel_id=1, source_target_pairs={{0,8},{1,25},{8,16},{9,1},{16,24},{17,9},{24,0},{25,17},{2,10},{3,... | collective-permute-start | bytes 1179656 | tf_op jit(solution)/shard_map/ppermute | solution.py:339
  13.9 12.1 %collective-permute-start.1 = (bf16[64,3072]{1,0:T(8,128)(2,1)S(1)}, bf16[64,3072]{1,0:T(8,128)(2,1)S(1)}, u32[]{:S(2)}, u32[]{:S(2)}) collective-permute-start(bf16[64,3072]{1,0:T(8,128)(2,1)S(1)} %copy-done.1), channel_id=1, source_target_pairs={{0,96},{1,33},{32,0},{33,65},{64,32},{65,97},{96,64},{97,1},{2,98}... | collective-permute-start | bytes 1179656 | tf_op jit(solution)/shard_map/ppermute | solution.py:339
  15.1 10.9 %collective-permute-start = (bf16[64,3072]{1,0:T(8,128)(2,1)S(1)}, bf16[64,3072]{1,0:T(8,128)(2,1)S(1)}, u32[]{:S(2)}, u32[]{:S(2)}) collective-permute-start(bf16[64,3072]{1,0:T(8,128)(2,1)S(1)} %copy-done.1), channel_id=1, source_target_pairs={{0,32},{1,97},{32,64},{33,1},{64,96},{65,33},{96,0},{97,65},{2,34}... | collective-permute-start | bytes 1179656 | tf_op jit(solution)/shard_map/ppermute | solution.py:339
  26.8 17.2 %collective-permute-start.9 = (bf16[128,3072]{1,0:T(8,128)(2,1)S(1)}, bf16[128,3072]{1,0:T(8,128)(2,1)S(1)}, u32[]{:S(2)}, u32[]{:S(2)}) collective-permute-start(bf16[128,3072]{1,0:T(8,128)(2,1)S(1)} %pad_maximum_fusion.1), channel_id=1, source_target_pairs={{0,8},{1,25},{8,16},{9,1},{16,24},{17,9},{24,0},{25,17},{2,10},{3,... | collective-permute-start | bytes 2359304 | tf_op jit(solution)/shard_map/ppermute | solution.py:339
  28.4 15.7 %collective-permute-start.7 = (bf16[128,3072]{1,0:T(8,128)(2,1)S(1)}, bf16[128,3072]{1,0:T(8,128)(2,1)S(1)}, u32[]{:S(2)}, u32[]{:S(2)}) collective-permute-start(bf16[128,3072]{1,0:T(8,128)(2,1)S(1)} %pad_maximum_fusion), channel_id=1, source_target_pairs={{0,32},{1,97},{32,64},{33,1},{64,96},{65,33},{96,0},{97,65},{2,34}... | collective-permute-start | bytes 2359304 | tf_op jit(solution)/shard_map/ppermute | solution.py:339
  29.4 14.7 %collective-permute-start.12 = (bf16[2,64,3072]{2,1,0:T(8,128)(2,1)S(1)}, bf16[2,64,3072]{2,1,0:T(8,128)(2,1)S(1)}, u32[]{:S(2)}, u32[]{:S(2)}) collective-permute-start(bf16[2,64,3072]{2,1,0:T(8,128)(2,1)S(1)} %collective-permute-done.6.refs_16_), channel_id=1, source_target_pairs={{0,2},{1,135},{2,4},{3,1},{4,6},{5,3},{6,128},{7,5},{128,130},{129... | collective-permute-start | bytes 2359304 | tf_op jit(solution)/shard_map/ppermute | solution.py:339
  32.0 11.8 %collective-permute-start.10 = (bf16[64,3072]{1,0:T(8,128)(2,1)S(1)}, bf16[64,3072]{1,0:T(8,128)(2,1)S(1)}, u32[]{:S(2)}, u32[]{:S(2)}) collective-permute-start(bf16[64,3072]{1,0:T(8,128)(2,1)S(1)} %pad_maximum_fusion.5), channel_id=1, source_target_pairs={{0,24},{1,9},{8,0},{9,17},{16,8},{17,25},{24,16},{25,1},{2,26},{3,... | collective-permute-start | bytes 1179656 | tf_op jit(solution)/shard_map/ppermute | solution.py:339
  32.1 11.9 %collective-permute-start.8 = (bf16[64,3072]{1,0:T(8,128)(2,1)S(1)}, bf16[64,3072]{1,0:T(8,128)(2,1)S(1)}, u32[]{:S(2)}, u32[]{:S(2)}) collective-permute-start(bf16[64,3072]{1,0:T(8,128)(2,1)S(1)} %pad_maximum_fusion.4), channel_id=1, source_target_pairs={{0,96},{1,33},{32,0},{33,65},{64,32},{65,97},{96,64},{97,1},{2,98}... | collective-permute-start | bytes 1179656 | tf_op jit(solution)/shard_map/ppermute | solution.py:339
  44.2 13.3 %collective-permute-start.15 = (bf16[96,3072]{1,0:T(8,128)(2,1)S(1)}, bf16[96,3072]{1,0:T(8,128)(2,1)S(1)}, u32[]{:S(2)}, u32[]{:S(2)}) collective-permute-start(bf16[96,3072]{1,0:T(8,128)(2,1)S(1)} %pad_maximum_fusion.3), channel_id=1, source_target_pairs={{0,8},{1,25},{8,16},{9,1},{16,24},{17,9},{24,0},{25,17},{2,10},{3,... | collective-permute-start | bytes 1769480 | tf_op jit(solution)/shard_map/ppermute | solution.py:339
  47.0 11.5 %collective-permute-start.17 = (bf16[2,64,3072]{2,1,0:T(8,128)(2,1)S(1)}, bf16[2,64,3072]{2,1,0:T(8,128)(2,1)S(1)}, u32[]{:S(2)}, u32[]{:S(2)}) collective-permute-start(bf16[2,64,3072]{2,1,0:T(8,128)(2,1)S(1)} %collective-permute-done.12.refs_17_), channel_id=1, source_target_pairs={{0,2},{1,135},{2,4},{3,1},{4,6},{5,3},{6,128},{7,5},{128,130},{129... | collective-permute-start | bytes 2359304 | tf_op jit(solution)/shard_map/ppermute | solution.py:339
  48.1 10.4 %collective-permute-start.13 = (bf16[96,3072]{1,0:T(8,128)(2,1)S(1)}, bf16[96,3072]{1,0:T(8,128)(2,1)S(1)}, u32[]{:S(2)}, u32[]{:S(2)}) collective-permute-start(bf16[96,3072]{1,0:T(8,128)(2,1)S(1)} %pad_maximum_fusion.2), channel_id=1, source_target_pairs={{0,32},{1,97},{32,64},{33,1},{64,96},{65,33},{96,0},{97,65},{2,34}... | collective-permute-start | bytes 1769480 | tf_op jit(solution)/shard_map/ppermute | solution.py:339
  49.1 8.2 %collective-permute-start.14 = (bf16[32,3072]{1,0:T(8,128)(2,1)S(1)}, bf16[32,3072]{1,0:T(8,128)(2,1)S(1)}, u32[]{:S(2)}, u32[]{:S(2)}) collective-permute-start(bf16[32,3072]{1,0:T(8,128)(2,1)S(1)} %slice.64), channel_id=1, source_target_pairs={{0,96},{1,33},{32,0},{33,65},{64,32},{65,97},{96,64},{97,1},{2,98}... | collective-permute-start | bytes 589832 | tf_op jit(solution)/shard_map/ppermute | solution.py:339
  49.8 7.7 %collective-permute-start.16 = (bf16[32,3072]{1,0:T(8,128)(2,1)S(1)}, bf16[32,3072]{1,0:T(8,128)(2,1)S(1)}, u32[]{:S(2)}, u32[]{:S(2)}) collective-permute-start(bf16[32,3072]{1,0:T(8,128)(2,1)S(1)} %slice.66), channel_id=1, source_target_pairs={{0,24},{1,9},{8,0},{9,17},{16,8},{17,25},{24,16},{25,1},{2,26},{3,... | collective-permute-start | bytes 589832 | tf_op jit(solution)/shard_map/ppermute | solution.py:339
  57.3 7.0 %collective-permute-start.21 = (bf16[2,64,3072]{2,1,0:T(8,128)(2,1)S(1)}, bf16[2,64,3072]{2,1,0:T(8,128)(2,1)S(1)}, u32[]{:S(2)}, u32[]{:S(2)}) collective-permute-start(bf16[2,64,3072]{2,1,0:T(8,128)(2,1)S(1)} %collective-permute-done.12.refs_17_), channel_id=1, source_target_pairs={{0,1},{1,0},{2,3},{3,2},{4,5},{5,4},{6,7},{7,6},{8,9},{9,8},{10,11... | collective-permute-start | bytes 2359304 | tf_op jit(solution)/shard_map/ppermute | solution.py:332
  58.5 9.6 %collective-permute-start.22 = (bf16[2,64,3072]{2,1,0:T(8,128)(2,1)S(1)}, bf16[2,64,3072]{2,1,0:T(8,128)(2,1)S(1)}, u32[]{:S(2)}, u32[]{:S(2)}) collective-permute-start(bf16[2,64,3072]{2,1,0:T(8,128)(2,1)S(1)} %collective-permute-done.17.refs_18_), channel_id=1, source_target_pairs={{0,1},{1,0},{2,3},{3,2},{4,5},{5,4},{6,7},{7,6},{8,9},{9,8},{10,11... | collective-permute-start | bytes 2359304 | tf_op jit(solution)/shard_map/ppermute | solution.py:332
  60.1 8.0 %collective-permute-start.20 = (bf16[64,3072]{1,0:T(8,128)(2,1)S(1)}, bf16[64,3072]{1,0:T(8,128)(2,1)S(1)}, u32[]{:S(2)}, u32[]{:S(2)}) collective-permute-start(bf16[64,3072]{1,0:T(8,128)(2,1)S(1)} %slice_bitcast_fusion), channel_id=1, source_target_pairs={{0,2},{1,135},{2,4},{3,1},{4,6},{5,3},{6,128},{7,5},{128,130},{129... | collective-permute-start | bytes 1179656 | tf_op jit(solution)/shard_map/ppermute | solution.py:339
  106.8 9.2 %collective-permute-start.32 = (f32[512,512]{1,0:T(8,128)}, f32[512,512]{1,0:T(8,128)S(1)}, u32[]{:S(2)}, u32[]{:S(2)}) collective-permute-start(f32[512,512]{1,0:T(8,128)} %get-tuple-element.78), channel_id=1, source_target_pairs={{0,1},{1,0},{2,3},{3,2},{4,5},{5,4},{6,7},{7,6},{8,9},{9,8},{10,11... | collective-permute-start | bytes 3145736 | tf_op jit(solution)/shard_map/ppermute | solution.py:332
  112.0 22.8 %all-to-all-start = ((bf16[16,64,512]{2,1,0:T(8,128)(2,1)}), bf16[16,64,512]{2,1,0:T(8,128)(2,1)S(1)}, u32[]{:S(2)}, u32[]{:S(2)}) async-start(bf16[16,64,512]{2,1,0:T(8,128)(2,1)} %bitcast.5), calls=%async_computation | async-start | bytes 2097152 | tf_op jit(solution)/shard_map/all_to_all | solution.py:413
  116.1 14.7 %collective-permute-start.33 = (bf16[128,512]{1,0:T(8,128)(2,1)S(1)}, bf16[128,512]{1,0:T(8,128)(2,1)S(1)}, u32[]{:S(2)}, u32[]{:S(2)}) collective-permute-start(bf16[128,512]{1,0:T(8,128)(2,1)S(1)} %get-tuple-element.80), channel_id=1, source_target_pairs={{0,2},{1,135},{2,4},{3,1},{4,6},{5,3},{6,128},{7,5},{128,130},{129... | collective-permute-start | bytes 393224 | tf_op jit(solution)/shard_map/ppermute | solution.py:339
  118.2 12.6 %collective-permute-start.34 = (bf16[128,512]{1,0:T(8,128)(2,1)S(1)}, bf16[128,512]{1,0:T(8,128)(2,1)S(1)}, u32[]{:S(2)}, u32[]{:S(2)}) collective-permute-start(bf16[128,512]{1,0:T(8,128)(2,1)S(1)} %get-tuple-element.81), channel_id=1, source_target_pairs={{0,4},{1,133},{2,6},{3,135},{4,128},{5,1},{6,130},{7,3},{128,132},... | collective-permute-start | bytes 393224 | tf_op jit(solution)/shard_map/ppermute | solution.py:339
  120.8 10.0 %collective-permute-start.35 = (bf16[128,512]{1,0:T(8,128)(2,1)S(1)}, bf16[128,512]{1,0:T(8,128)(2,1)S(1)}, u32[]{:S(2)}, u32[]{:S(2)}) collective-permute-start(bf16[128,512]{1,0:T(8,128)(2,1)S(1)} %get-tuple-element.82), channel_id=1, source_target_pairs={{0,6},{1,131},{2,128},{3,133},{4,130},{5,135},{6,132},{7,1},{128,1... | collective-permute-start | bytes 393224 | tf_op jit(solution)/shard_map/ppermute | solution.py:339
  122.6 8.2 %collective-permute-start.36 = (bf16[64,512]{1,0:T(8,128)(2,1)S(1)}, bf16[64,512]{1,0:T(8,128)(2,1)S(1)}, u32[]{:S(2)}, u32[]{:S(2)}) collective-permute-start(bf16[64,512]{1,0:T(8,128)(2,1)S(1)} %get-tuple-element.83), channel_id=1, source_target_pairs={{0,128},{1,129},{2,130},{3,131},{4,132},{5,133},{6,134},{7,135},{1... | collective-permute-start | bytes 196616 | tf_op jit(solution)/shard_map/ppermute | solution.py:339
  (17 other events, 61.2 us)

commit v3 on v2

--- a/solution.py
+++ b/solution.py
@@ -192,7 +192,7 @@
             scol_ref[here, :] = c_buf[here, 2 * width :]
             return 0
 
-        lax.fori_loop(0, m // 128, row_sums, 0)
+        lax.fori_loop(0, m // 128, row_sums, 0, unroll=4)
 
     return pl.pallas_call(
         kernel,
@@ -252,7 +252,7 @@
             acc[here, :] = tn(w_buf[:, here], srow_ref[...])
             return 0
 
-        lax.fori_loop(0, n // block, some_cols, 0)
+        lax.fori_loop(0, n // block, some_cols, 0, unroll=2)
 
         z = lax.axis_index(RING)
         sign = 1 - 2 * lax.axis_index("core")

time: 137 us -> 136 us (level)
  no operation moved by 1% of the time
where the time goes in v3:
time: 136 us; the launch traced here: 135 us
  starting transfers between devices  61.8 us (45%)
  waiting for transfers between devices  46.9 us (34%)
  Pallas kernels  23.1 us (17%)
    ppermute x22, waiting for transfers between devices, turn(): return lax.ppermute(x, axes, pairs)  38.1 us
    ppermute x22, starting transfers between devices, turn(): return lax.ppermute(x, axes, pairs)  34.7 us
    ppermute x9, starting transfers between devices, swap(): return lax.ppermute(x, 'core', [(0, 1), (1, 0)])  16.9 us
    pallas_call x1, Pallas kernels, logits(): pl.pallas_call(kernel, in_specs=[VMEM] * (n_rows + n_cols), out_specs=[VM...  14.2 us
    ppermute x7, waiting for transfers between devices, join_along(): return join(x, lax.ppermute(x, axis, [(i, i ^ step) for i in range(n)]))  7.32 us
    ppermute x7, starting transfers between devices, join_along(): return join(x, lax.ppermute(x, axis, [(i, i ^ step) for i in range(n)]))  6.27 us
    pallas_call x1, Pallas kernels, weights(): pl.pallas_call(kernel, in_specs=[VMEM] * 6, out_specs=[VMEM] * 3, out_sha...  5.85 us
    all_to_all x1, starting transfers between devices, local(): img_sent = lax.all_to_all(img.reshape(-1, share, ds), PLANE, 0, 0)  3.94 us
  transfers between devices with their start and end apart: 39, of which 17 were waited for; matrix products, arithmetic and copies ran while one was open for 0% of the time, Pallas kernels for 2%

profile of v3, /device:TPU:1, one launch (start us, length us, event | category | flops | bytes accessed | tf_op | source)
XLA Modules:
  0.0 135.2 jit_solution(6030104188262764633)
XLA Ops:
  0.6 3.3 %collective-permute-start.4 = (f32[64,1280]{1,0:T(8,128)}, f32[64,1280]{1,0:T(8,128)S(1)}, u32[]{:S(2)}, u32[]{:S(2)}) collective-permute-start(f32[64,1280]{1,0:T(8,128)} %bitcast.11), channel_id=1, source_target_pairs={{0,1},{1,0},{2,3},{3,2},{4,5},{5,4},{6,7},{7,6},{8,9},{9,8},{10,11... | collective-permute-start | bytes 983048 | tf_op jit(solution)/shard_map/ppermute | solution.py:332
  4.1 2.1 %pack.1 = (bf16[64,3072]{1,0:T(8,128)(2,1)}, bf16[64,3072]{1,0:T(8,128)(2,1)}) custom-call(f32[64,1280]{1,0:T(8,128)} %bitcast.10, bf16[64,512]{1,0:T(8,128)(2,1)} %bitcast.14, f32[64,1280]{1,0:T(8,128)} %bitcast.12, bf16[64,512]{1,0:T(8,128)(2,1)} %bitcast.16), custom_call_target="tpu_custom_call" | custom-call | tf_op jit(solution)/shard_map/pack/pallas_call | solution.py:66
  7.2 3.9 %collective-permute-start.6 = (bf16[2,64,3072]{2,1,0:T(8,128)(2,1)S(1)}, bf16[2,64,3072]{2,1,0:T(8,128)(2,1)S(1)}, u32[]{:S(2)}, u32[]{:S(2)}) collective-permute-start(bf16[2,64,3072]{2,1,0:T(8,128)(2,1)S(1)} %pair.1.refs_15_), channel_id=1, source_target_pairs={{0,2},{1,135},{2,4},{3,1},{4,6},{5,3},{6,128},{7,5},{128,130},{129... | collective-permute-start | bytes 2359304 | tf_op jit(solution)/shard_map/ppermute | solution.py:339
  16.6 6.8 %collective-permute-done.3.refs_4_ = bf16[64,3072]{1,0:T(8,128)(2,1)S(1)} collective-permute-done((bf16[64,3072]{1,0:T(8,128)(2,1)S(1)}, bf16[64,3072]{1,0:T(8,128)(2,1)S(1)}, u32[]{:S(2)}, u32[]{:S(2)}) %collective-permute-start.3) | collective-permute-done | bytes 393248 | tf_op jit(solution)/shard_map/ppermute | solution.py:339
  23.4 2.6 %collective-permute-done.1.refs_2_ = bf16[64,3072]{1,0:T(8,128)(2,1)S(1)} collective-permute-done((bf16[64,3072]{1,0:T(8,128)(2,1)S(1)}, bf16[64,3072]{1,0:T(8,128)(2,1)S(1)}, u32[]{:S(2)}, u32[]{:S(2)}) %collective-permute-start.1) | collective-permute-done | bytes 393248 | tf_op jit(solution)/shard_map/ppermute | solution.py:339
  29.4 2.6 %collective-permute-start.12 = (bf16[2,64,3072]{2,1,0:T(8,128)(2,1)S(1)}, bf16[2,64,3072]{2,1,0:T(8,128)(2,1)S(1)}, u32[]{:S(2)}, u32[]{:S(2)}) collective-permute-start(bf16[2,64,3072]{2,1,0:T(8,128)(2,1)S(1)} %collective-permute-done.6.refs_16_), channel_id=1, source_target_pairs={{0,2},{1,135},{2,4},{3,1},{4,6},{5,3},{6,128},{7,5},{128,130},{129... | collective-permute-start | bytes 2359304 | tf_op jit(solution)/shard_map/ppermute | solution.py:339
  32.2 11.7 %collective-permute-done.10.refs_8_ = bf16[64,3072]{1,0:T(8,128)(2,1)S(1)} collective-permute-done((bf16[64,3072]{1,0:T(8,128)(2,1)S(1)}, bf16[64,3072]{1,0:T(8,128)(2,1)S(1)}, u32[]{:S(2)}, u32[]{:S(2)}) %collective-permute-start.10) | collective-permute-done | bytes 393248 | tf_op jit(solution)/shard_map/ppermute | solution.py:339
  44.2 2.8 %collective-permute-start.15 = (bf16[96,3072]{1,0:T(8,128)(2,1)S(1)}, bf16[96,3072]{1,0:T(8,128)(2,1)S(1)}, u32[]{:S(2)}, u32[]{:S(2)}) collective-permute-start(bf16[96,3072]{1,0:T(8,128)(2,1)S(1)} %pad_maximum_fusion.3), channel_id=1, source_target_pairs={{0,8},{1,25},{8,16},{9,1},{16,24},{17,9},{24,0},{25,17},{2,10},{3,... | collective-permute-start | bytes 1769480 | tf_op jit(solution)/shard_map/ppermute | solution.py:339
  49.9 7.4 %collective-permute-done.14.refs_10_ = bf16[32,3072]{1,0:T(8,128)(2,1)S(1)} collective-permute-done((bf16[32,3072]{1,0:T(8,128)(2,1)S(1)}, bf16[32,3072]{1,0:T(8,128)(2,1)S(1)}, u32[]{:S(2)}, u32[]{:S(2)}) %collective-permute-start.14) | collective-permute-done | bytes 196640 | tf_op jit(solution)/shard_map/ppermute | solution.py:339
  60.1 2.5 %collective-permute-start.20 = (bf16[64,3072]{1,0:T(8,128)(2,1)S(1)}, bf16[64,3072]{1,0:T(8,128)(2,1)S(1)}, u32[]{:S(2)}, u32[]{:S(2)}) collective-permute-start(bf16[64,3072]{1,0:T(8,128)(2,1)S(1)} %slice_bitcast_fusion), channel_id=1, source_target_pairs={{0,2},{1,135},{2,4},{3,1},{4,6},{5,3},{6,128},{7,5},{128,130},{129... | collective-permute-start | bytes 1179656 | tf_op jit(solution)/shard_map/ppermute | solution.py:339
  64.4 3.2 %collective-permute-done.19.refs_14_ = bf16[32,3072]{1,0:T(8,128)(2,1)S(1)} collective-permute-done((bf16[32,3072]{1,0:T(8,128)(2,1)S(1)}, bf16[32,3072]{1,0:T(8,128)(2,1)S(1)}, u32[]{:S(2)}, u32[]{:S(2)}) %collective-permute-start.19) | collective-permute-done | bytes 196640 | tf_op jit(solution)/shard_map/ppermute | solution.py:339
  70.8 14.2 %logits.1 = (f32[1024,1024]{1,0:T(8,128)S(1)}, f32[1024,1024]{1,0:T(8,128)S(1)}, f32[2,1024]{1,0:T(2,128)S(1)}, f32[2,1024]{1,0:T(2,128)S(1)}, bf16[1024,512]{1,...) custom-call(bf16[64,3072]{1,0:T(8,128)(2,1)S(1)} %copy-done.1, bf16[64,3072]{1,0:T(8,128)(2,1)S(1)} %collective-permute-done.refs_1_, ...), custom_call_target="tpu_custom_call" | custom-call | flops 9126805504 | bytes 20971520 | tf_op jit(solution)/shard_map/logits/pallas_call | solution.py:197
  85.8 1.8 %collective-permute-done.24 = f32[2,1024]{1,0:T(2,128)S(1)} collective-permute-done((f32[2,1024]{1,0:T(2,128)S(1)}, f32[2,1024]{1,0:T(2,128)S(1)}, u32[]{:S(2)}, u32[]{:S(2)}) %collective-permute-start.24) | collective-permute-done | bytes 8224 | tf_op jit(solution)/shard_map/ppermute | solution.py:344
  89.1 2.3 %collective-permute-done.25 = f32[2,1024]{1,0:T(2,128)S(1)} collective-permute-done((f32[2,1024]{1,0:T(2,128)S(1)}, f32[2,1024]{1,0:T(2,128)S(1)}, u32[]{:S(2)}, u32[]{:S(2)}) %collective-permute-start.25) | collective-permute-done | bytes 8224 | tf_op jit(solution)/shard_map/ppermute | solution.py:344
  95.7 2.3 %collective-permute-start.31 = (f32[2,1024]{1,0:T(2,128)S(1)}, f32[2,1024]{1,0:T(2,128)S(1)}, u32[]{:S(2)}, u32[]{:S(2)}) collective-permute-start(f32[2,1024]{1,0:T(2,128)S(1)} %multiply_add_fusion.1), channel_id=1, source_target_pairs={{0,134},{2,132},{4,130},{6,128},{128,6},{130,4},{132,2},{134,0},{1... | collective-permute-start | bytes 24584 | tf_op jit(solution)/shard_map/ppermute | solution.py:344
  99.6 5.8 %weights.1 = (bf16[1024,512]{1,0:T(8,128)(2,1)}, f32[512,512]{1,0:T(8,128)S(1)}, f32[512,512]{1,0:T(8,128)}) custom-call(f32[1024,1024]{1,0:T(8,128)S(1)} %get-tuple-element.70.t_ref, f32[1024,1024]{1,0:T(8,128)S(1)} %get-tuple-element.71.s_ref, f32[2,1024]{1,0:T(2,128)S(1)} %multiply_add_fusion.4.row_ref, f32[2,1024]{1,0:T(2,128)S(1)} %multiply_add_fusion.col_ref, ...), custom_call_target="tpu_custom_call" | custom-call | flops 2147483648 | bytes 10485760 | tf_op jit(solution)/shard_map/weights/pallas_call | solution.py:275
  105.4 5.3 %collective-permute-start.32 = (f32[512,512]{1,0:T(8,128)}, f32[512,512]{1,0:T(8,128)S(1)}, u32[]{:S(2)}, u32[]{:S(2)}) collective-permute-start(f32[512,512]{1,0:T(8,128)} %get-tuple-element.78), channel_id=1, source_target_pairs={{0,1},{1,0},{2,3},{3,2},{4,5},{5,4},{6,7},{7,6},{8,9},{9,8},{10,11... | collective-permute-start | bytes 3145736 | tf_op jit(solution)/shard_map/ppermute | solution.py:332
  110.7 3.9 %all-to-all-start = ((bf16[16,64,512]{2,1,0:T(8,128)(2,1)}), bf16[16,64,512]{2,1,0:T(8,128)(2,1)S(1)}, u32[]{:S(2)}, u32[]{:S(2)}) async-start(bf16[16,64,512]{2,1,0:T(8,128)(2,1)} %bitcast.5), calls=%async_computation | async-start | bytes 2097152 | tf_op jit(solution)/shard_map/all_to_all | solution.py:413
  114.8 2.0 %collective-permute-start.33 = (bf16[128,512]{1,0:T(8,128)(2,1)S(1)}, bf16[128,512]{1,0:T(8,128)(2,1)S(1)}, u32[]{:S(2)}, u32[]{:S(2)}) collective-permute-start(bf16[128,512]{1,0:T(8,128)(2,1)S(1)} %get-tuple-element.80), channel_id=1, source_target_pairs={{0,2},{1,135},{2,4},{3,1},{4,6},{5,3},{6,128},{7,5},{128,130},{129... | collective-permute-start | bytes 393224 | tf_op jit(solution)/shard_map/ppermute | solution.py:339
  116.8 2.7 %collective-permute-start.34 = (bf16[128,512]{1,0:T(8,128)(2,1)S(1)}, bf16[128,512]{1,0:T(8,128)(2,1)S(1)}, u32[]{:S(2)}, u32[]{:S(2)}) collective-permute-start(bf16[128,512]{1,0:T(8,128)(2,1)S(1)} %get-tuple-element.81), channel_id=1, source_target_pairs={{0,4},{1,133},{2,6},{3,135},{4,128},{5,1},{6,130},{7,3},{128,132},... | collective-permute-start | bytes 393224 | tf_op jit(solution)/shard_map/ppermute | solution.py:339
  119.5 1.7 %collective-permute-start.35 = (bf16[128,512]{1,0:T(8,128)(2,1)S(1)}, bf16[128,512]{1,0:T(8,128)(2,1)S(1)}, u32[]{:S(2)}, u32[]{:S(2)}) collective-permute-start(bf16[128,512]{1,0:T(8,128)(2,1)S(1)} %get-tuple-element.82), channel_id=1, source_target_pairs={{0,6},{1,131},{2,128},{3,133},{4,130},{5,135},{6,132},{7,1},{128,1... | collective-permute-start | bytes 393224 | tf_op jit(solution)/shard_map/ppermute | solution.py:339
  121.2 3.7 %collective-permute-start.36 = (bf16[64,512]{1,0:T(8,128)(2,1)S(1)}, bf16[64,512]{1,0:T(8,128)(2,1)S(1)}, u32[]{:S(2)}, u32[]{:S(2)}) collective-permute-start(bf16[64,512]{1,0:T(8,128)(2,1)S(1)} %get-tuple-element.83), channel_id=1, source_target_pairs={{0,128},{1,129},{2,130},{3,131},{4,132},{5,133},{6,134},{7,135},{1... | collective-permute-start | bytes 196616 | tf_op jit(solution)/shard_map/ppermute | solution.py:339
  125.0 4.5 %collective-permute-done.36 = bf16[64,512]{1,0:T(8,128)(2,1)S(1)} collective-permute-done((bf16[64,512]{1,0:T(8,128)(2,1)S(1)}, bf16[64,512]{1,0:T(8,128)(2,1)S(1)}, u32[]{:S(2)}, u32[]{:S(2)}) %collective-permute-start.36) | collective-permute-done | bytes 65568 | tf_op jit(solution)/shard_map/ppermute | solution.py:339
  129.6 3.9 %collective-permute-start.37 = (f32[64,512]{1,0:T(8,128)S(1)}, f32[64,512]{1,0:T(8,128)S(1)}, u32[]{:S(2)}, u32[]{:S(2)}) collective-permute-start(f32[64,512]{1,0:T(8,128)S(1)} %slice_add_fusion), channel_id=1, source_target_pairs={{0,1},{1,0},{2,3},{3,2},{4,5},{5,4},{6,7},{7,6},{8,9},{9,8},{10,11... | collective-permute-start | bytes 393224 | tf_op jit(solution)/shard_map/ppermute | solution.py:332
  (95 shorter events, 31.1 us)
Async XLA Ops:
  7.2 18.8 %collective-permute-start.6 = (bf16[2,64,3072]{2,1,0:T(8,128)(2,1)S(1)}, bf16[2,64,3072]{2,1,0:T(8,128)(2,1)S(1)}, u32[]{:S(2)}, u32[]{:S(2)}) collective-permute-start(bf16[2,64,3072]{2,1,0:T(8,128)(2,1)S(1)} %pair.1.refs_15_), channel_id=1, source_target_pairs={{0,2},{1,135},{2,4},{3,1},{4,6},{5,3},{6,128},{7,5},{128,130},{129... | collective-permute-start | bytes 2359304 | tf_op jit(solution)/shard_map/ppermute | solution.py:339
  11.2 12.2 %collective-permute-start.3 = (bf16[64,3072]{1,0:T(8,128)(2,1)S(1)}, bf16[64,3072]{1,0:T(8,128)(2,1)S(1)}, u32[]{:S(2)}, u32[]{:S(2)}) collective-permute-start(bf16[64,3072]{1,0:T(8,128)(2,1)S(1)} %copy-done.1), channel_id=1, source_target_pairs={{0,24},{1,9},{8,0},{9,17},{16,8},{17,25},{24,16},{25,1},{2,26},{3,... | collective-permute-start | bytes 1179656 | tf_op jit(solution)/shard_map/ppermute | solution.py:339
  12.5 10.9 %collective-permute-start.2 = (bf16[64,3072]{1,0:T(8,128)(2,1)S(1)}, bf16[64,3072]{1,0:T(8,128)(2,1)S(1)}, u32[]{:S(2)}, u32[]{:S(2)}) collective-permute-start(bf16[64,3072]{1,0:T(8,128)(2,1)S(1)} %copy-done.1), channel_id=1, source_target_pairs={{0,8},{1,25},{8,16},{9,1},{16,24},{17,9},{24,0},{25,17},{2,10},{3,... | collective-permute-start | bytes 1179656 | tf_op jit(solution)/shard_map/ppermute | solution.py:339
  13.9 12.1 %collective-permute-start.1 = (bf16[64,3072]{1,0:T(8,128)(2,1)S(1)}, bf16[64,3072]{1,0:T(8,128)(2,1)S(1)}, u32[]{:S(2)}, u32[]{:S(2)}) collective-permute-start(bf16[64,3072]{1,0:T(8,128)(2,1)S(1)} %copy-done.1), channel_id=1, source_target_pairs={{0,96},{1,33},{32,0},{33,65},{64,32},{65,97},{96,64},{97,1},{2,98}... | collective-permute-start | bytes 1179656 | tf_op jit(solution)/shard_map/ppermute | solution.py:339
  15.1 10.9 %collective-permute-start = (bf16[64,3072]{1,0:T(8,128)(2,1)S(1)}, bf16[64,3072]{1,0:T(8,128)(2,1)S(1)}, u32[]{:S(2)}, u32[]{:S(2)}) collective-permute-start(bf16[64,3072]{1,0:T(8,128)(2,1)S(1)} %copy-done.1), channel_id=1, source_target_pairs={{0,32},{1,97},{32,64},{33,1},{64,96},{65,33},{96,0},{97,65},{2,34}... | collective-permute-start | bytes 1179656 | tf_op jit(solution)/shard_map/ppermute | solution.py:339
  26.8 17.2 %collective-permute-start.9 = (bf16[128,3072]{1,0:T(8,128)(2,1)S(1)}, bf16[128,3072]{1,0:T(8,128)(2,1)S(1)}, u32[]{:S(2)}, u32[]{:S(2)}) collective-permute-start(bf16[128,3072]{1,0:T(8,128)(2,1)S(1)} %pad_maximum_fusion.1), channel_id=1, source_target_pairs={{0,8},{1,25},{8,16},{9,1},{16,24},{17,9},{24,0},{25,17},{2,10},{3,... | collective-permute-start | bytes 2359304 | tf_op jit(solution)/shard_map/ppermute | solution.py:339
  28.4 15.7 %collective-permute-start.7 = (bf16[128,3072]{1,0:T(8,128)(2,1)S(1)}, bf16[128,3072]{1,0:T(8,128)(2,1)S(1)}, u32[]{:S(2)}, u32[]{:S(2)}) collective-permute-start(bf16[128,3072]{1,0:T(8,128)(2,1)S(1)} %pad_maximum_fusion), channel_id=1, source_target_pairs={{0,32},{1,97},{32,64},{33,1},{64,96},{65,33},{96,0},{97,65},{2,34}... | collective-permute-start | bytes 2359304 | tf_op jit(solution)/shard_map/ppermute | solution.py:339
  29.4 14.7 %collective-permute-start.12 = (bf16[2,64,3072]{2,1,0:T(8,128)(2,1)S(1)}, bf16[2,64,3072]{2,1,0:T(8,128)(2,1)S(1)}, u32[]{:S(2)}, u32[]{:S(2)}) collective-permute-start(bf16[2,64,3072]{2,1,0:T(8,128)(2,1)S(1)} %collective-permute-done.6.refs_16_), channel_id=1, source_target_pairs={{0,2},{1,135},{2,4},{3,1},{4,6},{5,3},{6,128},{7,5},{128,130},{129... | collective-permute-start | bytes 2359304 | tf_op jit(solution)/shard_map/ppermute | solution.py:339
  32.0 11.8 %collective-permute-start.10 = (bf16[64,3072]{1,0:T(8,128)(2,1)S(1)}, bf16[64,3072]{1,0:T(8,128)(2,1)S(1)}, u32[]{:S(2)}, u32[]{:S(2)}) collective-permute-start(bf16[64,3072]{1,0:T(8,128)(2,1)S(1)} %pad_maximum_fusion.5), channel_id=1, source_target_pairs={{0,24},{1,9},{8,0},{9,17},{16,8},{17,25},{24,16},{25,1},{2,26},{3,... | collective-permute-start | bytes 1179656 | tf_op jit(solution)/shard_map/ppermute | solution.py:339
  32.1 11.9 %collective-permute-start.8 = (bf16[64,3072]{1,0:T(8,128)(2,1)S(1)}, bf16[64,3072]{1,0:T(8,128)(2,1)S(1)}, u32[]{:S(2)}, u32[]{:S(2)}) collective-permute-start(bf16[64,3072]{1,0:T(8,128)(2,1)S(1)} %pad_maximum_fusion.4), channel_id=1, source_target_pairs={{0,96},{1,33},{32,0},{33,65},{64,32},{65,97},{96,64},{97,1},{2,98}... | collective-permute-start | bytes 1179656 | tf_op jit(solution)/shard_map/ppermute | solution.py:339
  44.2 13.3 %collective-permute-start.15 = (bf16[96,3072]{1,0:T(8,128)(2,1)S(1)}, bf16[96,3072]{1,0:T(8,128)(2,1)S(1)}, u32[]{:S(2)}, u32[]{:S(2)}) collective-permute-start(bf16[96,3072]{1,0:T(8,128)(2,1)S(1)} %pad_maximum_fusion.3), channel_id=1, source_target_pairs={{0,8},{1,25},{8,16},{9,1},{16,24},{17,9},{24,0},{25,17},{2,10},{3,... | collective-permute-start | bytes 1769480 | tf_op jit(solution)/shard_map/ppermute | solution.py:339
  47.0 11.5 %collective-permute-start.17 = (bf16[2,64,3072]{2,1,0:T(8,128)(2,1)S(1)}, bf16[2,64,3072]{2,1,0:T(8,128)(2,1)S(1)}, u32[]{:S(2)}, u32[]{:S(2)}) collective-permute-start(bf16[2,64,3072]{2,1,0:T(8,128)(2,1)S(1)} %collective-permute-done.12.refs_17_), channel_id=1, source_target_pairs={{0,2},{1,135},{2,4},{3,1},{4,6},{5,3},{6,128},{7,5},{128,130},{129... | collective-permute-start | bytes 2359304 | tf_op jit(solution)/shard_map/ppermute | solution.py:339
  48.1 10.4 %collective-permute-start.13 = (bf16[96,3072]{1,0:T(8,128)(2,1)S(1)}, bf16[96,3072]{1,0:T(8,128)(2,1)S(1)}, u32[]{:S(2)}, u32[]{:S(2)}) collective-permute-start(bf16[96,3072]{1,0:T(8,128)(2,1)S(1)} %pad_maximum_fusion.2), channel_id=1, source_target_pairs={{0,32},{1,97},{32,64},{33,1},{64,96},{65,33},{96,0},{97,65},{2,34}... | collective-permute-start | bytes 1769480 | tf_op jit(solution)/shard_map/ppermute | solution.py:339
  49.1 8.2 %collective-permute-start.14 = (bf16[32,3072]{1,0:T(8,128)(2,1)S(1)}, bf16[32,3072]{1,0:T(8,128)(2,1)S(1)}, u32[]{:S(2)}, u32[]{:S(2)}) collective-permute-start(bf16[32,3072]{1,0:T(8,128)(2,1)S(1)} %slice.64), channel_id=1, source_target_pairs={{0,96},{1,33},{32,0},{33,65},{64,32},{65,97},{96,64},{97,1},{2,98}... | collective-permute-start | bytes 589832 | tf_op jit(solution)/shard_map/ppermute | solution.py:339
  49.8 7.7 %collective-permute-start.16 = (bf16[32,3072]{1,0:T(8,128)(2,1)S(1)}, bf16[32,3072]{1,0:T(8,128)(2,1)S(1)}, u32[]{:S(2)}, u32[]{:S(2)}) collective-permute-start(bf16[32,3072]{1,0:T(8,128)(2,1)S(1)} %slice.66), channel_id=1, source_target_pairs={{0,24},{1,9},{8,0},{9,17},{16,8},{17,25},{24,16},{25,1},{2,26},{3,... | collective-permute-start | bytes 589832 | tf_op jit(solution)/shard_map/ppermute | solution.py:339
  57.3 7.0 %collective-permute-start.21 = (bf16[2,64,3072]{2,1,0:T(8,128)(2,1)S(1)}, bf16[2,64,3072]{2,1,0:T(8,128)(2,1)S(1)}, u32[]{:S(2)}, u32[]{:S(2)}) collective-permute-start(bf16[2,64,3072]{2,1,0:T(8,128)(2,1)S(1)} %collective-permute-done.12.refs_17_), channel_id=1, source_target_pairs={{0,1},{1,0},{2,3},{3,2},{4,5},{5,4},{6,7},{7,6},{8,9},{9,8},{10,11... | collective-permute-start | bytes 2359304 | tf_op jit(solution)/shard_map/ppermute | solution.py:332
  58.5 9.6 %collective-permute-start.22 = (bf16[2,64,3072]{2,1,0:T(8,128)(2,1)S(1)}, bf16[2,64,3072]{2,1,0:T(8,128)(2,1)S(1)}, u32[]{:S(2)}, u32[]{:S(2)}) collective-permute-start(bf16[2,64,3072]{2,1,0:T(8,128)(2,1)S(1)} %collective-permute-done.17.refs_18_), channel_id=1, source_target_pairs={{0,1},{1,0},{2,3},{3,2},{4,5},{5,4},{6,7},{7,6},{8,9},{9,8},{10,11... | collective-permute-start | bytes 2359304 | tf_op jit(solution)/shard_map/ppermute | solution.py:332
  60.1 8.0 %collective-permute-start.20 = (bf16[64,3072]{1,0:T(8,128)(2,1)S(1)}, bf16[64,3072]{1,0:T(8,128)(2,1)S(1)}, u32[]{:S(2)}, u32[]{:S(2)}) collective-permute-start(bf16[64,3072]{1,0:T(8,128)(2,1)S(1)} %slice_bitcast_fusion), channel_id=1, source_target_pairs={{0,2},{1,135},{2,4},{3,1},{4,6},{5,3},{6,128},{7,5},{128,130},{129... | collective-permute-start | bytes 1179656 | tf_op jit(solution)/shard_map/ppermute | solution.py:339
  105.4 9.2 %collective-permute-start.32 = (f32[512,512]{1,0:T(8,128)}, f32[512,512]{1,0:T(8,128)S(1)}, u32[]{:S(2)}, u32[]{:S(2)}) collective-permute-start(f32[512,512]{1,0:T(8,128)} %get-tuple-element.78), channel_id=1, source_target_pairs={{0,1},{1,0},{2,3},{3,2},{4,5},{5,4},{6,7},{7,6},{8,9},{9,8},{10,11... | collective-permute-start | bytes 3145736 | tf_op jit(solution)/shard_map/ppermute | solution.py:332
  110.7 22.9 %all-to-all-start = ((bf16[16,64,512]{2,1,0:T(8,128)(2,1)}), bf16[16,64,512]{2,1,0:T(8,128)(2,1)S(1)}, u32[]{:S(2)}, u32[]{:S(2)}) async-start(bf16[16,64,512]{2,1,0:T(8,128)(2,1)} %bitcast.5), calls=%async_computation | async-start | bytes 2097152 | tf_op jit(solution)/shard_map/all_to_all | solution.py:413
  114.8 14.7 %collective-permute-start.33 = (bf16[128,512]{1,0:T(8,128)(2,1)S(1)}, bf16[128,512]{1,0:T(8,128)(2,1)S(1)}, u32[]{:S(2)}, u32[]{:S(2)}) collective-permute-start(bf16[128,512]{1,0:T(8,128)(2,1)S(1)} %get-tuple-element.80), channel_id=1, source_target_pairs={{0,2},{1,135},{2,4},{3,1},{4,6},{5,3},{6,128},{7,5},{128,130},{129... | collective-permute-start | bytes 393224 | tf_op jit(solution)/shard_map/ppermute | solution.py:339
  116.8 12.7 %collective-permute-start.34 = (bf16[128,512]{1,0:T(8,128)(2,1)S(1)}, bf16[128,512]{1,0:T(8,128)(2,1)S(1)}, u32[]{:S(2)}, u32[]{:S(2)}) collective-permute-start(bf16[128,512]{1,0:T(8,128)(2,1)S(1)} %get-tuple-element.81), channel_id=1, source_target_pairs={{0,4},{1,133},{2,6},{3,135},{4,128},{5,1},{6,130},{7,3},{128,132},... | collective-permute-start | bytes 393224 | tf_op jit(solution)/shard_map/ppermute | solution.py:339
  119.5 10.0 %collective-permute-start.35 = (bf16[128,512]{1,0:T(8,128)(2,1)S(1)}, bf16[128,512]{1,0:T(8,128)(2,1)S(1)}, u32[]{:S(2)}, u32[]{:S(2)}) collective-permute-start(bf16[128,512]{1,0:T(8,128)(2,1)S(1)} %get-tuple-element.82), channel_id=1, source_target_pairs={{0,6},{1,131},{2,128},{3,133},{4,130},{5,135},{6,132},{7,1},{128,1... | collective-permute-start | bytes 393224 | tf_op jit(solution)/shard_map/ppermute | solution.py:339
  121.2 8.2 %collective-permute-start.36 = (bf16[64,512]{1,0:T(8,128)(2,1)S(1)}, bf16[64,512]{1,0:T(8,128)(2,1)S(1)}, u32[]{:S(2)}, u32[]{:S(2)}) collective-permute-start(bf16[64,512]{1,0:T(8,128)(2,1)S(1)} %get-tuple-element.83), channel_id=1, source_target_pairs={{0,128},{1,129},{2,130},{3,131},{4,132},{5,133},{6,134},{7,135},{1... | collective-permute-start | bytes 196616 | tf_op jit(solution)/shard_map/ppermute | solution.py:339
  (17 other events, 60.7 us)
